TPU v7x, 128 devices: a whole 4x4x4 slice. The times are simulated.
128 devices in a mesh: dp: 8 (over z, y_lo), tensor: 16 (over y_hi, x, core).
Axes of the slice: x: 4, y: 4 (y_hi: 2, y_lo: 2; y = y_hi * 2 + y_lo), z: 4, core: 2. Of those that a mesh axis runs over, the one named last changes fastest.
Arguments:
- x_rows: bfloat16 [2048, 4096], P('dp'), may hold values from -6 to 6
- lengths: int32 [16], P('dp'), may hold values from 1 to 128, 1280 in all
- routes: int32 [2048, 2], P('dp'), may hold values from 0 to 7, all different within a row; in each aligned block of 256 rows (0 to 255, 256 to 511, ...) at most 96 rows name the same one
- conv_state: bfloat16 [16, 3, 8192], P('dp', None, 'tensor'), may hold values from -6 to 6
- ssm_state: float32 [16, 16, 8192], P('dp', None, 'tensor'), may hold values from -6 to 6
- norm1_gain: float32 [4096], replicated, may hold values from 0.5 to 1.5
- in_x: bfloat16 [4096, 8192], P('dp', 'tensor'), may hold values from -0.09375 to 0.09375
- in_z: bfloat16 [4096, 8192], P('dp', 'tensor'), may hold values from -0.09375 to 0.09375
- conv_w: float32 [4, 8192], P(None, 'tensor'), may hold values from -3 to 3
- conv_b: float32 [8192], P('tensor'), may hold values from -3 to 3
- x_dt: bfloat16 [8192, 512], P('tensor'), may hold values from -0.0625 to 0.0625
- x_bc: bfloat16 [8192, 32], P('tensor'), may hold values from -0.0625 to 0.0625
- dt_proj: bfloat16 [512, 8192], P(None, 'tensor'), may hold values from -0.25 to 0.25
- dt_bias: float32 [8192], P('tensor'), may hold values from -5 to -2
- decay_rate: float32 [16, 8192], P(None, 'tensor'), may hold values from 0.05 to 4
- skip: float32 [8192], P('tensor'), may hold values from 0.5 to 1.5
- out_w: bfloat16 [8192, 4096], P('tensor', 'dp'), may hold values from -0.0625 to 0.0625
- norm2_gain: float32 [4096], replicated, may hold values from 0.5 to 1.5
- router: bfloat16 [4096, 8], replicated, may hold values from -0.09375 to 0.09375
- w_gate: bfloat16 [8, 4096, 12288], P('dp', None, 'tensor'), may hold values from -0.09375 to 0.09375
- w_up: bfloat16 [8, 4096, 12288], P('dp', None, 'tensor'), may hold values from -0.09375 to 0.09375
- w_down: bfloat16 [8, 12288, 4096], P('dp', 'tensor'), may hold values from -0.0546875 to 0.0546875
Outputs:
- out_rows: bfloat16 [2048, 4096], P('dp')
- ssm_final: float32 [16, 16, 8192], P('dp', None, 'tensor')
Inputs may be any that keep to these rules, and one draw needn't show every extreme that they name: `lengths`: every request has at least one valid token, and some request has all 128. `routes`: a token's 2 experts differ; in each aligned block of 256 rows (the tokens of one request group) no expert is named by more than 96 rows, and some block names some expert exactly 96 times.
All inputs are finite; a program needn't handle non-finite values. No bound on the sum of `lengths` on one device may be relied on, other than what follows from the above.
Results may differ from a plain program's by a relative error of at most 0.023.
Values may be sent and summed in bfloat16 or wider, within the bound.
No kernel may reach another device: no remote copies, remote signals or barrier semaphores. Data moves between devices by JAX's collectives and lax.ppermute only.
A program may use at most 128 MiB of HBM per device.

v0:
```python
import jax
import jax.numpy as jnp
from jax import lax
from jax.sharding import PartitionSpec as P

EXPERTS = 8
TOP = 2


def norm_rows(values, gain):
    values = values.astype(jnp.float32)
    mean_square = jnp.mean(values * values, axis=-1, keepdims=True)
    return values * lax.rsqrt(mean_square + 1e-05) * gain


def slot_tables(picks, expert_count, capacity):
    row_count, top_count = picks.shape
    onehot = (picks[:, :, None] == jnp.arange(expert_count, dtype=jnp.int32)).astype(jnp.int32)
    flat_hits = onehot.reshape(row_count * top_count, expert_count)
    before = jnp.cumsum(flat_hits, axis=0) - flat_hits
    rank_of = jnp.sum(before * flat_hits, axis=1).reshape(row_count, top_count)
    placed = rank_of[:, :, None] == jnp.arange(capacity, dtype=jnp.int32)
    return ((onehot[:, :, :, None] > 0) & placed[:, :, None, :]).astype(jnp.bfloat16)


def block_scan(start_state, step_size, signal, entry_gain, read_gain, decay_rate):
    requests, block_length, channels = step_size.shape
    piece_len = 16
    piece_count = block_length // piece_len
    empty_out = jnp.zeros((requests, block_length, channels), jnp.float32)

    def one_piece(carry, piece_index):
        state, outputs = carry
        begin = piece_index * piece_len
        step_piece = lax.dynamic_slice_in_dim(step_size, begin, piece_len, 1)
        signal_piece = lax.dynamic_slice_in_dim(signal, begin, piece_len, 1)
        entry_piece = lax.dynamic_slice_in_dim(entry_gain, begin, piece_len, 1)
        read_piece = lax.dynamic_slice_in_dim(read_gain, begin, piece_len, 1)
        rows_out = []
        for offset in range(piece_len):
            step_now = step_piece[:, offset]
            drive_now = step_now * signal_piece[:, offset]
            state = (
                jnp.exp(-step_now[:, None, :] * decay_rate) * state
                + drive_now[:, None, :] * entry_piece[:, offset][:, :, None]
            )
            rows_out.append(jnp.sum(read_piece[:, offset][:, :, None] * state, axis=1))
        piece_out = jnp.stack(rows_out, axis=1)
        outputs = lax.dynamic_update_slice_in_dim(outputs, piece_out, begin, 1)
        return ((state, outputs), None)

    (final_state, outputs), _ = lax.scan(
        one_piece, (start_state, empty_out), jnp.arange(piece_count, dtype=jnp.int32)
    )
    return (final_state, outputs)


def per_device(
    x_rows,
    lengths,
    routes,
    conv_state,
    ssm_state,
    norm1_gain,
    in_x,
    in_z,
    conv_w,
    conv_b,
    x_dt,
    x_bc,
    dt_proj,
    dt_bias,
    decay_rate,
    skip,
    out_w,
    norm2_gain,
    router,
    w_gate,
    w_up,
    w_down,
):
    row_count, model_width = x_rows.shape
    requests, state_count, channels = ssm_state.shape
    expert_count = router.shape[1]
    block_length = row_count // requests
    capacity = max(2, 3 * row_count * TOP // (2 * EXPERTS))
    normed = norm_rows(x_rows, norm1_gain).astype(jnp.bfloat16)
    x_inner = jnp.dot(
        normed, lax.all_gather(in_x, "dp", axis=0, tiled=True), preferred_element_type=jnp.float32
    )
    z_inner = jnp.dot(
        normed, lax.all_gather(in_z, "dp", axis=0, tiled=True), preferred_element_type=jnp.float32
    )
    x_inner = x_inner.astype(jnp.bfloat16)
    z_gate = z_inner.astype(jnp.bfloat16)
    history = jnp.concatenate(
        [conv_state, x_inner.reshape(requests, block_length, channels)], axis=1
    ).astype(jnp.float32)
    filter_tap_count = conv_w.shape[0]
    conv_sum = conv_b + sum(
        (
            conv_w[shift_index] * history[:, shift_index : shift_index + block_length]
            for shift_index in range(filter_tap_count)
        )
    )
    conv_out = jax.nn.silu(conv_sum).astype(jnp.bfloat16).reshape(row_count, channels)
    low_part = jnp.dot(conv_out, x_dt, preferred_element_type=jnp.float32)
    gain_part = jnp.dot(conv_out, x_bc, preferred_element_type=jnp.float32)
    low_sum, bc_sum = lax.psum((low_part, gain_part), "tensor")
    step_low = low_sum.astype(jnp.bfloat16)
    valid_mask = (jnp.arange(block_length, dtype=jnp.int32)[None, :] < lengths[:, None]).astype(
        jnp.float32
    )
    step_size = jax.nn.softplus(
        jnp.dot(step_low, dt_proj, preferred_element_type=jnp.float32) + dt_bias
    )
    step_size = step_size.reshape(requests, block_length, channels) * valid_mask[:, :, None]
    entry_gain = bc_sum[:, :state_count].reshape(requests, block_length, state_count)
    read_gain = bc_sum[:, state_count:].reshape(requests, block_length, state_count)
    signal = conv_out.reshape(requests, block_length, channels).astype(jnp.float32)
    final_state, scan_out = block_scan(
        ssm_state, step_size, signal, entry_gain, read_gain, decay_rate
    )
    mixer_y = scan_out + skip * signal
    gate_act = jax.nn.silu(z_gate.reshape(requests, block_length, channels).astype(jnp.float32))
    gated = (
        (mixer_y * gate_act * valid_mask[:, :, None])
        .astype(jnp.bfloat16)
        .reshape(row_count, channels)
    )
    out_full = lax.all_gather(out_w, "dp", axis=1, tiled=True)
    mixer = lax.psum(
        jnp.dot(gated, out_full, preferred_element_type=jnp.float32).astype(jnp.bfloat16), "tensor"
    ).astype(jnp.float32)
    hidden = (x_rows.astype(jnp.float32) + mixer).astype(jnp.bfloat16)
    unit = norm_rows(hidden, norm2_gain).astype(jnp.bfloat16)
    tables = slot_tables(routes, expert_count, capacity)
    outgoing = jnp.einsum("rkec,rd->ecd", tables, unit, preferred_element_type=jnp.float32).astype(
        jnp.bfloat16
    )
    arriving = lax.all_to_all(outgoing, "dp", split_axis=0, concat_axis=1, tiled=True)
    flat_rows = arriving[0]
    gate_part = jnp.dot(flat_rows, w_gate[0], preferred_element_type=jnp.float32)
    up_part = jnp.dot(flat_rows, w_up[0], preferred_element_type=jnp.float32)
    active = (jax.nn.silu(gate_part) * up_part).astype(jnp.bfloat16)
    results = [jnp.dot(active, w_down[0], preferred_element_type=jnp.float32).astype(jnp.bfloat16)]
    partial_value_sum = jnp.stack(results, axis=0)
    logits = jnp.dot(unit, router, preferred_element_type=jnp.float32)
    chosen = routes[:, :, None] == jnp.arange(expert_count, dtype=jnp.int32)
    gates = jnp.sum(jnp.where(chosen, jax.nn.sigmoid(logits)[:, None, :], 0.0), axis=-1)
    summed = lax.psum(partial_value_sum.astype(jnp.float32).astype(jnp.bfloat16), "tensor")
    back_rows = lax.all_to_all(summed, "dp", split_axis=1, concat_axis=0, tiled=True)
    expert_out = jnp.einsum(
        "rkec,ecd->rkd", tables, back_rows, preferred_element_type=jnp.float32
    ).astype(jnp.bfloat16)
    out_rows = (
        hidden.astype(jnp.float32)
        + jnp.sum(gates[:, :, None] * expert_out.astype(jnp.float32), axis=1)
    ).astype(jnp.bfloat16)
    return (out_rows, final_state)


def solution(mesh):
    return jax.shard_map(
        per_device,
        mesh=mesh,
        in_specs=(
            P("dp", None),
            P("dp"),
            P("dp", None),
            P("dp", None, "tensor"),
            P("dp", None, "tensor"),
            P(),
            P("dp", "tensor"),
            P("dp", "tensor"),
            P(None, "tensor"),
            P("tensor"),
            P("tensor", None),
            P("tensor", None),
            P(None, "tensor"),
            P("tensor"),
            P(None, "tensor"),
            P("tensor"),
            P("tensor", "dp"),
            P(),
            P(),
            P("dp", None, "tensor"),
            P("dp", None, "tensor"),
            P("dp", "tensor", None),
        ),
        out_specs=(P("dp", None), P("dp", None, "tensor")),
        check_vma=False,
    )
```

profile of v0, /device:TPU:1, one launch (start us, length us, event | category | flops | bytes accessed | tf_op | source)
XLA Modules:
  0.0 1004.4 jit_solution(17682531355366295239)
XLA Ops:
  10.3 2.1 fusion.24
  13.8 89.8 %all-gather.4.cloned.1.call-done = bf16[4096,512]{1,0:T(8,128)(2,1)} async-done(((bf16[512,512]{1,0:T(8,128)(2,1)}), bf16[4096,512]{1,0:T(8,128)(2,1)}) %all-gather.4.cloned.1.call-update) | async-done | bytes 4194320 | tf_op jit(solution)/shard_map/all_gather | solution.py:89
  103.6 4.1 convolution_convert_fusion.4
  109.5 71.2 %all-reduce.8 = (bf16[256,512]{1,0:T(8,128)(2,1)S(1)}, f32[256,32]{0,1:T(8,128)S(1)}) all-reduce(f32[256,512]{1,0:T(8,128)S(1)} %fusion.63, f32[256,32]{0,1:T(8,128)S(1)} %fusion.64), channel_id=1, replica_groups=mesh['dp'=8,'tensor'=16] {'tensor'}, use_global_device_ids=true, to_apply=%region_1.2 | all-reduce | flops 139264 | bytes 851968 | tf_op jit(solution)/shard_map/psum | solution.py:109
  182.9 222.5 %while.12 = (s32[]{:T(128)}, f32[2,16,512]{2,1,0:T(8,128)S(1)}, f32[2,128,512]{2,1,0:T(8,128)S(1)}, s32[8]{0:T(128)}, f32[2,128,512]{2,1,0:T(8,128)}, /*index=5*...) while((s32[]{:T(128)}, f32[2,16,512]{2,1,0:T(8,128)S(1)}, ...), condition=%wide.region_20.21_spmd, body=%wide.region_3.20_spmd.sunk | while | flops 2375701 | bytes 1988711 | solution.py:52
  189.5 2.4 constant_dynamic-slice_fusion.67
  217.4 2.2 constant_dynamic-slice_fusion.67
  245.0 2.5 constant_dynamic-slice_fusion.67
  273.0 2.2 constant_dynamic-slice_fusion.67
  300.6 2.5 constant_dynamic-slice_fusion.67
  328.5 2.3 constant_dynamic-slice_fusion.67
  356.2 2.2 constant_dynamic-slice_fusion.67
  383.9 2.5 constant_dynamic-slice_fusion.67
  405.5 3.5 convolution_convert_fusion.3
  409.3 4.8 convolution_convert_fusion.2
  416.8 142.6 %all-reduce.5.cloned.1.call-done = bf16[256,4096]{1,0:T(8,128)(2,1)} async-done(((bf16[256,4096]{1,0:T(8,128)(2,1)}), bf16[256,4096]{1,0:T(8,128)(2,1)}) %all-reduce.5.cloned.1.call-update) | async-done | bytes 2097168 | tf_op jit(solution)/shard_map/psum | solution.py:132
  559.4 3.2 fusion.28
  562.6 1.9 convolution_convert_fusion.1
  564.6 74.6 %all_to_all.21 = bf16[8,96,4096]{2,1,0:T(8,128)(2,1)S(1)} all-to-all(bf16[8,96,4096]{2,1,0:T(8,128)(2,1)S(1)} %convolution_convert_fusion.1), channel_id=1, replica_groups=mesh['dp'=8,'tensor'=16] {'dp'}, dimensions={0} | all-to-all | bytes 12582912 | tf_op jit(solution)/shard_map/all_to_all | solution.py:141
  639.2 5.1 fusion.19
  644.2 5.2 multiply_convert_fusion
  649.5 9.9 fusion.21
  659.4 154.8 %all-reduce.7.cloned.1.call-done = bf16[1,768,4096]{2,1,0:T(8,128)(2,1)} async-done(((bf16[1,768,4096]{2,1,0:T(8,128)(2,1)}), bf16[1,768,4096]{2,1,0:T(8,128)(2,1)}) %all-reduce.7.cloned.1.call-update) | async-done | bytes 6291472 | tf_op jit(solution)/shard_map/psum | solution.py:151
  814.2 15.5 %copy.206 = bf16[1,768,4096]{2,0,1:T(2,128)(2,1)} copy(bf16[1,768,4096]{2,1,0:T(8,128)(2,1)} %all-reduce.7.cloned.1.call-done) | data formatting | bytes 12582912 | tf_op jit(solution)/shard_map/psum | solution.py:151
  830.3 40.0 %reduce.2 = bf16[768,4096]{1,0:T(8,128)(2,1)} reduce(bf16[768,1,4096]{2,1,0:T(2,128)(2,1)} %bitcast.263, bf16[]{:T(256)} %broadcast.99), dimensions={1}, to_apply=%bitcast.163.reduce_sub_computation | reduce | bytes 12582914
  870.2 9.4 reshape.156
  879.6 13.5 %all-to-all-start.1 = ((bf16[8,2,196608]{2,1,0:T(2,128)(2,1)}), bf16[8,2,196608]{2,1,0:T(2,128)(2,1)}, u32[]{:S(2)}, u32[]{:S(2)}) async-start(bf16[8,2,196608]{2,1,0:T(2,128)(2,1)} %reshape.156), calls=%async_computation.1 | async-start | bytes 12582912 | tf_op jit(solution)/shard_map/all_to_all | solution.py:152
  893.9 69.2 %all-to-all-done.1 = bf16[8,2,196608]{2,1,0:T(2,128)(2,1)} async-done(((bf16[8,2,196608]{2,1,0:T(2,128)(2,1)}), bf16[8,2,196608]{2,1,0:T(2,128)(2,1)}, u32[]{:S(2)}, u32[]{:S(2)}) %all-to-all-start.1) | async-done | bytes 6291488 | tf_op jit(solution)/shard_map/all_to_all | solution.py:152
  963.1 10.9 %reshape.157 = bf16[768,1,4096]{2,1,0:T(2,128)(2,1)} reshape(bf16[8,2,196608]{2,1,0:T(2,128)(2,1)} %all-to-all-done.1) | data formatting | bytes 12582912
  974.0 14.4 %copy.60 = bf16[1,768,4096]{2,1,0:T(8,128)(2,1)} copy(bf16[1,768,4096]{2,0,1:T(2,128)(2,1)} %bitcast.262) | data formatting | bytes 12582912
  988.4 7.3 multiply_reduce_fusion.16
  995.7 2.0 fusion.31
  (674 shorter events, 208.6 us)
Async XLA Ops:
  7.2 101.9 %copy-start = (bf16[512,512]{1,0:T(8,128)(2,1)S(1)}, bf16[512,512]{1,0:T(8,128)(2,1)}, u32[]{:S(2)}) copy-start(bf16[512,512]{1,0:T(8,128)(2,1)} %param.34) | copy-start | bytes 1572868
  7.2 96.5 %all-gather.4.cloned.1.call-start = ((), (), s32[]{:S(2)}) async-start(), calls=%async_computation.2 | async-start | bytes 4718592 | tf_op jit(solution)/shard_map/all_gather | solution.py:89
  7.9 397.5 %all-gather.6.cloned.1.call-start = ((), (), s32[]{:S(2)}) async-start(), calls=%async_computation.3 | async-start | bytes 4718592 | tf_op jit(solution)/shard_map/all_gather | solution.py:92
  8.7 400.6 %all-gather.8.cloned.1.call-start = ((), (), s32[]{:S(2)}) async-start(), calls=%async_computation.4 | async-start | bytes 4718592 | tf_op jit(solution)/shard_map/all_gather | solution.py:131
  9.4 550.0 %all-reduce.5.cloned.1.call-start = ((), (), s32[]{:S(2)}) async-start(), calls=%async_computation.5 | async-start | bytes 4194304 | tf_op jit(solution)/shard_map/psum | solution.py:132
  12.4 95.4 %copy-start.13 = (f32[256]{0:T(256)}, f32[256]{0:T(256)S(1)}, u32[]{:S(2)}) copy-start(f32[256]{0:T(256)S(1)} %add_rsqrt_fusion.1) | copy-start | bytes 3076
  13.8 167.5 %copy-start.9 = (f32[2,128]{1,0:T(2,128)}, f32[2,128]{1,0:T(2,128)S(1)}, u32[]{:S(2)}) copy-start(f32[2,128]{1,0:T(2,128)S(1)} %compare_convert_fusion) | copy-start | bytes 3076
  13.8 94.1 %copy-start.11 = (f32[512]{0:T(512)S(1)}, f32[512]{0:T(512)}, u32[]{:S(2)}) copy-start(f32[512]{0:T(512)} %param.33) | copy-start | bytes 6148
  107.8 1.6 copy-start.6
  107.8 73.0 %copy-start.14 = (bf16[512,512]{1,0:T(8,128)(2,1)S(1)}, bf16[512,512]{1,0:T(8,128)(2,1)}, u32[]{:S(2)}) copy-start(bf16[512,512]{1,0:T(8,128)(2,1)} %param.36) | copy-start | bytes 1572868
  107.8 73.0 %copy-start.16 = (f32[512]{0:T(512)S(1)}, f32[512]{0:T(512)}, u32[]{:S(2)}) copy-start(f32[512]{0:T(512)} %param.37) | copy-start | bytes 6148
  107.9 75.0 %copy-start.2 = (f32[16,512]{1,0:T(8,128)S(1)}, f32[16,512]{1,0:T(8,128)}, u32[]{:S(2)}) copy-start(f32[16,512]{1,0:T(8,128)} %param.38) | copy-start | bytes 98308
  107.9 75.0 %copy-start.5 = (f32[2,16,512]{2,1,0:T(8,128)S(1)}, f32[2,16,512]{2,1,0:T(8,128)}, u32[]{:S(2)}) copy-start(f32[2,16,512]{2,1,0:T(8,128)} %param.28) | copy-start | bytes 196612
  182.9 222.5 %copy-start.3 = (bf16[256,4096]{1,0:T(8,128)(2,1)S(1)}, bf16[256,4096]{1,0:T(8,128)(2,1)}, u32[]{:S(2)}) copy-start(bf16[256,4096]{1,0:T(8,128)(2,1)} %param.24) | copy-start | bytes 6291460
  405.4 3.6 copy-start.4
  405.4 3.6 copy-start.10
  405.4 3.6 copy-start.12
  409.2 5.1 copy-start.7
  414.0 148.5 %copy-start.8 = (f32[4096]{0:T(1024)S(1)}, f32[4096]{0:T(1024)}, u32[]{:S(2)}) copy-start(f32[4096]{0:T(1024)} %param.41) | copy-start | bytes 49156
  414.1 400.2 %all-reduce.7.cloned.1.call-start = ((), (), s32[]{:S(2)}) async-start(), calls=%async_computation.6 | async-start | bytes 12582912 | tf_op jit(solution)/shard_map/psum | solution.py:151
  562.6 76.5 %slice-start = ((s8[6291456]{0:T(1024)(128)(4,1)}), s8[4194304]{0:T(1024)(128)(4,1)S(1)}, s32[]{:S(2)}) async-start(s8[6291456]{0:T(1024)(128)(4,1)} %bitcast.321), calls=%async_computation.7 | async-start | bytes 8388608
  564.6 74.6 %slice-start.1 = ((s8[6291456]{0:T(1024)(128)(4,1)}), s8[2097152]{0:T(1024)(128)(4,1)S(1)}, s32[]{:S(2)}) async-start(s8[6291456]{0:T(1024)(128)(4,1)} %bitcast.321), calls=%async_computation.8 | async-start | bytes 4194304
  564.6 79.6 %slice-start.2 = ((s8[6291456]{0:T(1024)(128)(4,1)}), s8[4194304]{0:T(1024)(128)(4,1)S(1)}, s32[]{:S(2)}) async-start(s8[6291456]{0:T(1024)(128)(4,1)} %bitcast.323), calls=%async_computation.9 | async-start | bytes 8388608
  639.2 5.1 slice-start.3
  879.6 13.5 %copy-start.15 = (bf16[4096,8]{0,1:T(8,128)(2,1)S(1)}, bf16[4096,8]{0,1:T(8,128)(2,1)}, u32[]{:S(2)}) copy-start(bf16[4096,8]{0,1:T(8,128)(2,1)} %param.42) | copy-start | bytes 196612
  879.6 83.5 %all-to-all-start.1 = ((bf16[8,2,196608]{2,1,0:T(2,128)(2,1)}), bf16[8,2,196608]{2,1,0:T(2,128)(2,1)}, u32[]{:S(2)}, u32[]{:S(2)}) async-start(bf16[8,2,196608]{2,1,0:T(2,128)(2,1)} %reshape.156), calls=%async_computation.1 | async-start | bytes 12582912 | tf_op jit(solution)/shard_map/all_to_all | solution.py:152
  988.4 9.3 copy-start.1
Sparse Core Ops, SparseCore 0:
  9.7 93.9 all-gather.3
  105.3 97.0 all-gather.5
  204.0 89.7 all-gather.7
  414.2 145.1 all-reduce.4
  659.5 154.6 all-reduce.6
where the time goes:
time: 1010 us; the launch traced here: 1000 us
  waiting for transfers between devices  459 us (45%)
  local copies, waits for them, and re-layouts  217 us (21%)
  blocking collectives  146 us (14%)
  other arithmetic  103 us (10%)
  matrix products  43.6 us (4%)
  between operations  14.5 us (1%)
  starting transfers between devices  14 us (1%)
    psum x1, waiting for transfers between devices, per_device(): lax.psum(partial_value_sum.astype(jnp.float32).astype(jnp.bfloat16), 'ten...  155 us
    psum x1, waiting for transfers between devices, per_device(): lax.psum(jnp.dot(gated, out_full, preferred_element_type=jnp.float32).ast...  143 us
    while x256, local copies, waits for them, and re-layouts  112 us
    all_gather x1, waiting for transfers between devices, per_device(): lax.all_gather(in_x, 'dp', axis=0, tiled=True)  89.8 us
    all_to_all x1, blocking collectives, per_device(): lax.all_to_all(outgoing, 'dp', split_axis=0, concat_axis=1, tiled=True)  74.6 us
    psum x1, blocking collectives, per_device(): low_sum, bc_sum = lax.psum((low_part, gain_part), 'tensor')  71.2 us
    all_to_all x1, waiting for transfers between devices, per_device(): lax.all_to_all(summed, 'dp', split_axis=1, concat_axis=0, tiled=True)  69.2 us
    unnamed x3, other arithmetic  40 us
  transfers between devices with their start and end apart: 6, of which 4 were waited for; matrix products, arithmetic and copies ran while one was open for 23% of the time, Pallas kernels for 0%

commit v1 on v0

v1 whole, which is shorter than its diff:
```python
import jax
import jax.numpy as jnp
from jax import lax
from jax.sharding import Mesh
from jax.sharding import PartitionSpec as P
from jax.experimental import pallas as pl
from jax.experimental.pallas import tpu as pltpu

F32 = jnp.float32
BF16 = jnp.bfloat16
DP = ("z", "ylo")
TENSOR = ("yhi", "x", "core")
CHIPS = ("yhi", "x")
EPS = 1e-05
LOG2E = 1.4426950408889634


def params(megabytes=48):
    return pltpu.CompilerParams(vmem_limit_bytes=megabytes << 20)


def call(body, scalars, grid, in_specs, out_specs, out_shape, scratch=(), cost=None):
    spec = pltpu.PrefetchScalarGridSpec(
        num_scalar_prefetch=len(scalars),
        grid=grid,
        in_specs=in_specs,
        out_specs=out_specs,
        scratch_shapes=scratch,
    )
    return pl.pallas_call(
        body, grid_spec=spec, out_shape=out_shape, compiler_params=params(), cost_estimate=cost
    )


def exchange(value, axes):
    return lax.all_to_all(value, axes, split_axis=0, concat_axis=0, tiled=True)


def spread(value):
    return exchange(jnp.broadcast_to(value[None], (8,) + value.shape), CHIPS)


def swap_core(value):
    return lax.ppermute(value, "core", [(0, 1), (1, 0)])


def sigmoid(value):
    return 1.0 / (1.0 + jnp.exp(-value))


def silu(value):
    return value * sigmoid(value)


def norm_split(core, x_rows, gain):
    def body(core_ref, x_ref, gain_ref, out_ref):
        values = x_ref[...].astype(F32)
        scale = lax.rsqrt(jnp.mean(values * values, axis=-1, keepdims=True) + EPS)
        normed = (values * scale * gain_ref[...]).astype(BF16)
        for piece in range(8):
            out_ref[piece] = normed[:, piece * 512 : piece * 512 + 512]

    return call(
        body,
        (core,),
        (1,),
        [
            pl.BlockSpec((128, 4096), lambda i, c: (c[0], 0)),
            pl.BlockSpec((1, 4096), lambda i, c: (0, 0)),
        ],
        pl.BlockSpec((8, 128, 512), lambda i, c: (0, 0, 0)),
        jax.ShapeDtypeStruct((8, 128, 512), BF16),
    )(core, x_rows, gain)


def partial_product(own, other, weight):
    def body(own_ref, other_ref, w_ref, out_ref):
        weight_now = w_ref[...]
        for slot, rows_ref in enumerate((own_ref, other_ref)):
            out_ref[:, slot] = (
                jnp.dot(rows_ref[...].reshape(512, 512), weight_now, preferred_element_type=F32)
                .astype(BF16)
                .reshape(4, 128, 512)
            )

    rows = pl.BlockSpec((4, 128, 512), lambda i: (i, 0, 0))
    return call(
        body,
        (),
        (2,),
        [rows, rows, pl.BlockSpec((512, 512), lambda i: (0, 0))],
        pl.BlockSpec((4, 2, 128, 512), lambda i: (i, 0, 0, 0)),
        jax.ShapeDtypeStruct((8, 2, 128, 512), BF16),
    )(own, other, weight)


def conv_project(core, parts, history, conv_w, conv_b, weight):
    def body(core_ref, parts_ref, hist_ref, cw_ref, cb_ref, w_ref, conv_ref, low_ref, line):
        x_inner = jnp.sum(parts_ref[:, 0].astype(F32), axis=0).astype(BF16).astype(F32)
        line[0:8] = hist_ref[0]
        line[8:136] = x_inner
        total = cb_ref[...] + cw_ref[3:4] * x_inner
        for tap in range(3):
            total = total + cw_ref[tap : tap + 1] * line[5 + tap : 133 + tap]
        conv = silu(total).astype(BF16)
        conv_ref[0] = conv
        low_ref[0] = jnp.dot(conv, w_ref[...], preferred_element_type=F32).astype(BF16)

    return call(
        body,
        (core,),
        (2,),
        [
            pl.BlockSpec((8, 1, 128, 512), lambda r, c: (0, r ^ c[0], 0, 0)),
            pl.BlockSpec((1, 8, 512), lambda r, c: (r, 0, 0)),
            pl.BlockSpec((4, 512), lambda r, c: (0, 0)),
            pl.BlockSpec((1, 512), lambda r, c: (0, 0)),
            pl.BlockSpec((512, 640), lambda r, c: (0, 0)),
        ],
        [
            pl.BlockSpec((1, 128, 512), lambda r, c: (r, 0, 0)),
            pl.BlockSpec((1, 128, 640), lambda r, c: (r ^ c[0], 0, 0)),
        ],
        [
            jax.ShapeDtypeStruct((2, 128, 512), BF16),
            jax.ShapeDtypeStruct((2, 128, 640), BF16),
        ],
        (pltpu.VMEM((136, 512), F32),),
    )(core, parts, history, conv_w, conv_b, weight)


def scan_gate(core, lengths, low_own, low_other, z_parts, conv, dt_proj, dt_bias, decay, skip, state):
    def body(
        core_ref,
        len_ref,
        own_ref,
        other_ref,
        z_ref,
        conv_ref,
        dtp_ref,
        dtb_ref,
        decay_ref,
        skip_ref,
        state_ref,
        gated_ref,
        final_ref,
        step_s,
        drive_s,
        trail_s,
        dec_s,
    ):
        dec_s[...] = decay_ref[...] * (-LOG2E)
        lane = lax.broadcasted_iota(jnp.int32, (128, 128), 1)
        row = lax.broadcasted_iota(jnp.int32, (128, 128), 0)
        pick_entry = (row == lane % 16).astype(BF16)
        pick_read = (row == 16 + lane % 16).astype(BF16)
        diagonal = ((lane // 16) == (row % 8)).astype(F32)
        position = lax.broadcasted_iota(jnp.int32, (128, 512), 0)
        reads = []
        for slot, low_ref in enumerate((own_ref, other_ref)):
            request = core_ref[0] ^ slot
            mask = (position < len_ref[request]).astype(F32)
            raw = jnp.dot(low_ref[:, 0:512], dtp_ref[...], preferred_element_type=F32) + dtb_ref[...]
            step = (jnp.maximum(raw, 0.0) + jnp.log(1.0 + jnp.exp(-jnp.abs(raw)))) * mask
            step_s[slot] = step
            drive = (step * conv_ref[request].astype(F32)).astype(BF16)
            tail = low_ref[:, 512:640]
            entry = (jnp.dot(tail, pick_entry, preferred_element_type=F32) * diagonal).astype(BF16)
            reads.append(
                (jnp.dot(tail, pick_read, preferred_element_type=F32) * diagonal).astype(BF16)
            )
            for piece in range(8):
                for half in range(2):
                    at = piece * 16 + half * 8
                    keep = (
                        lax.broadcasted_iota(jnp.int32, (16, 128), 0) // 8 == half
                    ).astype(BF16)
                    drive_s[slot, at * 16 : at * 16 + 128] = lax.dot_general(
                        entry[piece * 16 : piece * 16 + 16] * keep,
                        drive[piece * 16 : piece * 16 + 16],
                        (((0,), (0,)), ((), ())),
                        preferred_element_type=F32,
                    )

        def advance(block, held):
            held = list(held)
            base = pl.multiple_of(block * 8, 8)
            for slot in range(2):
                steps = step_s[slot, pl.ds(base, 8)]
                now = held[slot]
                for offset in range(8):
                    rows = pl.ds(pl.multiple_of(block * 128 + offset * 16, 16), 16)
                    now = jnp.exp2(steps[offset : offset + 1] * dec_s[...]) * now + drive_s[slot, rows]
                    trail_s[slot, rows] = now.astype(BF16)
                held[slot] = now
            return tuple(held)

        first = tuple(state_ref[core_ref[0] ^ slot] for slot in range(2))
        last = lax.fori_loop(0, 16, advance, first)
        for slot in range(2):
            request = core_ref[0] ^ slot
            final_ref[request] = last[slot]
            outs = []
            for piece in range(16):
                outs.append(
                    jnp.dot(
                        reads[slot][piece * 8 : piece * 8 + 8],
                        trail_s[slot, piece * 128 : piece * 128 + 128],
                        preferred_element_type=F32,
                    )
                )
            mask = (position < len_ref[request]).astype(F32)
            mixed = jnp.concatenate(outs, axis=0) + skip_ref[...] * conv_ref[request].astype(F32)
            z_gate = jnp.sum(z_ref[:, slot].astype(F32), axis=0).astype(BF16).astype(F32)
            gated_ref[request] = (mixed * silu(z_gate) * mask).astype(BF16)

    def whole(*shape):
        return pl.BlockSpec(shape, lambda i, c, n: (0,) * len(shape))

    return call(
        body,
        (core, lengths),
        (1,),
        [
            whole(128, 640),
            whole(128, 640),
            whole(8, 2, 128, 512),
            whole(2, 128, 512),
            whole(512, 512),
            whole(1, 512),
            whole(16, 512),
            whole(1, 512),
            whole(2, 16, 512),
        ],
        [whole(2, 128, 512), whole(2, 16, 512)],
        [
            jax.ShapeDtypeStruct((2, 128, 512), BF16),
            jax.ShapeDtypeStruct((2, 16, 512), F32),
        ],
        (
            pltpu.VMEM((2, 128, 512), F32),
            pltpu.VMEM((2, 2048, 512), F32),
            pltpu.VMEM((2, 2048, 512), BF16),
            pltpu.VMEM((16, 512), F32),
        ),
    )(core, lengths, low_own, low_other, z_parts, conv, dt_proj, dt_bias, decay, skip, state)


def half_product(target, rows, weight, weight_spec, received=None):
    row_count, depth = rows.shape

    def body(target_ref, rows_ref, w_ref, *refs):
        out_ref = refs[-1]
        product = jnp.dot(
            rows_ref[...], w_ref[...].reshape(depth, 512), preferred_element_type=F32
        )
        for side in range(2):
            value = product[:, side * 256 : side * 256 + 256]
            if received is not None:
                value = value + refs[0][side].astype(F32)
            out_ref[side] = value.astype(BF16)

    blocks = pl.BlockSpec((2, row_count, 256), lambda i, t: (i, 0, 0))
    operands = (target, rows, weight) + (() if received is None else (received,))
    return call(
        body,
        (target,),
        (4,),
        [pl.BlockSpec((row_count, depth), lambda i, t: (0, 0)), weight_spec]
        + ([] if received is None else [blocks]),
        blocks,
        jax.ShapeDtypeStruct((8, row_count, 256), BF16),
    )(*operands)


def tables_of(routes_t):
    expert = lax.broadcasted_iota(jnp.int32, (8, 256), 0)
    picks = [(expert == routes_t[k : k + 1]) for k in range(2)]
    counts = (picks[0] | picks[1]).astype(BF16)
    earlier = (
        lax.broadcasted_iota(jnp.int32, (256, 256), 0)
        < lax.broadcasted_iota(jnp.int32, (256, 256), 1)
    ).astype(BF16)
    before = jnp.dot(counts, earlier, preferred_element_type=F32)
    place = before + 96.0 * expert.astype(F32)
    slot_row = lax.broadcasted_iota(jnp.int32, (768, 256), 0)
    hit = None
    for pick in picks:
        slot = jnp.sum(jnp.where(pick, place, 0.0), axis=0, keepdims=True).astype(jnp.int32)
        mine = slot_row == slot
        hit = mine if hit is None else hit | mine
    return hit.astype(BF16)


def hidden_dispatch(block, parts, x_rows, routes_t):
    def body(block_ref, parts_ref, x_ref, routes_ref, hidden_ref, out_ref):
        mixer = jnp.sum(parts_ref[...].astype(F32), axis=0)
        hidden = (x_ref[...].astype(F32) + mixer).astype(BF16)
        hidden_ref[...] = hidden
        out_ref[...] = jnp.dot(
            tables_of(routes_ref[...]), hidden, preferred_element_type=F32
        ).astype(BF16)

    return call(
        body,
        (block,),
        (1,),
        [
            pl.BlockSpec((8, 256, 256), lambda i, b: (0, 0, 0)),
            pl.BlockSpec((256, 256), lambda i, b: (0, b[0])),
            pl.BlockSpec((2, 256), lambda i, b: (0, 0)),
        ],
        [
            pl.BlockSpec((256, 256), lambda i, b: (0, 0)),
            pl.BlockSpec((768, 256), lambda i, b: (0, 0)),
        ],
        [
            jax.ShapeDtypeStruct((256, 256), BF16),
            jax.ShapeDtypeStruct((768, 256), BF16),
        ],
    )(block, parts, x_rows, routes_t)


def gate_up(core, own, other, gain, router_row, w_gate, w_up):
    def body(core_ref, own_ref, other_ref, gain_ref, router_ref, wg_ref, wu_ref, out_ref, g_s, u_s, sq_s, lo_s):
        step = pl.program_id(0)

        def work(rows_ref):
            scaled, squares, logits = [], None, None
            for piece in range(4):
                at = slice(piece * 256, piece * 256 + 256)
                value = rows_ref[piece].astype(F32)
                square = value * value
                square = square[:, 0:128] + square[:, 128:256]
                squares = square if squares is None else squares + square
                times = (value * gain_ref[:, at]).astype(BF16)
                scaled.append(times)
                logit = times.astype(F32) * router_ref[:, at]
                logit = logit[:, 0:128] + logit[:, 128:256]
                logits = logit if logits is None else logits + logit
            units = jnp.concatenate(scaled, axis=1)
            gate = jnp.dot(units, wg_ref[...], preferred_element_type=F32)
            up = jnp.dot(units, wu_ref[...], preferred_element_type=F32)

            @pl.when(step == 0)
            def _():
                g_s[...] = gate
                u_s[...] = up
                sq_s[...] = squares
                lo_s[...] = logits

            @pl.when(step > 0)
            def _():
                g_s[...] += gate
                u_s[...] += up
                sq_s[...] += squares
                lo_s[...] += logits

        @pl.when(step < 2)
        def _():
            work(own_ref)

        @pl.when(step >= 2)
        def _():
            work(other_ref)

        @pl.when(step == 3)
        def _():
            scale = lax.rsqrt(jnp.sum(sq_s[...], axis=1, keepdims=True) * (1.0 / 4096.0) + EPS)
            weight = sigmoid(jnp.sum(lo_s[...], axis=1, keepdims=True) * scale)
            out_ref[...] = (silu(g_s[...] * scale) * (u_s[...] * (scale * weight))).astype(BF16)

    def at(i, c):
        return jnp.where(i < 2, c[0] * 2 + i, (1 - c[0]) * 2 + i - 2)

    return call(
        body,
        (core,),
        (4,),
        [
            pl.BlockSpec((4, 768, 256), lambda i, c: (jnp.minimum(i, 1), 0, 0)),
            pl.BlockSpec((4, 768, 256), lambda i, c: (jnp.maximum(i - 2, 0), 0, 0)),
            pl.BlockSpec((1, 1024), lambda i, c: (0, at(i, c))),
            pl.BlockSpec((1, 1024), lambda i, c: (0, at(i, c))),
            pl.BlockSpec((1024, 768), lambda i, c: (at(i, c), 0)),
            pl.BlockSpec((1024, 768), lambda i, c: (at(i, c), 0)),
        ],
        pl.BlockSpec((768, 768), lambda i, c: (0, 0)),
        jax.ShapeDtypeStruct((768, 768), BF16),
        (
            pltpu.VMEM((768, 768), F32),
            pltpu.VMEM((768, 768), F32),
            pltpu.VMEM((768, 128), F32),
            pltpu.VMEM((768, 128), F32),
        ),
    )(core, own, other, gain, router_row, w_gate, w_up)


def sum_parts(parts):
    def body(parts_ref, out_ref):
        out_ref[...] = jnp.sum(parts_ref[...].astype(F32), axis=0).astype(BF16)

    return call(
        body,
        (),
        (4,),
        [pl.BlockSpec((8, 192, 256), lambda i: (0, i, 0))],
        pl.BlockSpec((192, 256), lambda i: (i, 0)),
        jax.ShapeDtypeStruct((768, 256), BF16),
    )(parts)


def combine(hidden, back, routes_t):
    def body(hidden_ref, back_ref, routes_ref, out_ref):
        mixed = lax.dot_general(
            tables_of(routes_ref[...]),
            back_ref[...],
            (((0,), (0,)), ((), ())),
            preferred_element_type=F32,
        )
        out_ref[...] = (hidden_ref[...].astype(F32) + mixed).astype(BF16)

    return call(
        body,
        (),
        (1,),
        [
            pl.BlockSpec((256, 256), lambda i: (0, 0)),
            pl.BlockSpec((768, 256), lambda i: (0, 0)),
            pl.BlockSpec((2, 256), lambda i: (0, 0)),
        ],
        pl.BlockSpec((256, 256), lambda i: (0, 0)),
        jax.ShapeDtypeStruct((256, 256), BF16),
    )(hidden, back, routes_t)


def assemble(core, own, other):
    def body(core_ref, own_ref, other_ref, out_ref):
        for side, ref in enumerate((own_ref, other_ref)):

            @pl.when(pl.program_id(0) == side)
            def _():
                for piece in range(4):
                    out_ref[:, piece * 256 : piece * 256 + 256] = ref[piece]

    return call(
        body,
        (core,),
        (2, 2),
        [
            pl.BlockSpec((4, 256, 256), lambda s, i, c: (jnp.where(s == 0, i, 1), 0, 0)),
            pl.BlockSpec((4, 256, 256), lambda s, i, c: (jnp.where(s == 0, 0, i), 0, 0)),
        ],
        pl.BlockSpec((256, 1024), lambda s, i, c: (0, (c[0] ^ s) * 2 + i)),
        jax.ShapeDtypeStruct((256, 4096), BF16),
    )(core, own, other)


def per_device(
    x_rows,
    lengths,
    routes,
    conv_state,
    ssm_state,
    norm1_gain,
    in_x,
    in_z,
    conv_w,
    conv_b,
    x_dt,
    x_bc,
    dt_proj,
    dt_bias,
    decay_rate,
    skip,
    out_w,
    norm2_gain,
    router,
    w_gate,
    w_up,
    w_down,
):
    core_at = lax.axis_index("core").astype(jnp.int32)
    core = core_at.reshape(1)
    away = (1 - core_at).reshape(1)
    chip_at = lax.axis_index(CHIPS).astype(jnp.int32)
    block = (core_at * 8 + chip_at).reshape(1)
    expert_at = lax.axis_index(DP).astype(jnp.int32)

    out_full = lax.all_gather(out_w, DP, axis=0, tiled=True).reshape(8, 512, 512)
    low_weight = jnp.concatenate([x_dt, x_bc, jnp.zeros((512, 96), BF16)], axis=1)
    history = jnp.pad(conv_state.astype(F32), ((0, 0), (5, 0), (0, 0)))
    routes_t = routes.T
    router_row = lax.dynamic_slice(router, (0, expert_at), (4096, 1)).astype(F32).reshape(1, 4096)

    own = exchange(norm_split(core, x_rows, norm1_gain.reshape(1, 4096)), DP)
    other = swap_core(own)
    x_parts = exchange(partial_product(own, other, in_x), DP)
    z_parts = exchange(partial_product(own, other, in_z), DP)
    conv, low = conv_project(core, x_parts, history, conv_w, conv_b.reshape(1, 512), low_weight)
    low_pair = (low[0].astype(F32) + swap_core(low[1]).astype(F32)).astype(BF16)
    low_sum = jnp.sum(exchange(low_pair.reshape(8, 16, 640), CHIPS).astype(F32), axis=0).astype(BF16)
    low_own = spread(low_sum).reshape(128, 640)
    low_other = swap_core(low_own)
    gated, final = scan_gate(
        core,
        lengths,
        low_own,
        low_other,
        z_parts,
        conv,
        dt_proj,
        dt_bias.reshape(1, 512),
        decay_rate,
        skip.reshape(1, 512),
        ssm_state,
    )
    gated = gated.reshape(256, 512)
    out_spec = pl.BlockSpec((1, 512, 512), lambda i, t: (t[0] * 4 + i, 0, 0))
    far = swap_core(half_product(away, gated, out_full, out_spec))
    mixer_parts = exchange(half_product(core, gated, out_full, out_spec, far), CHIPS)
    hidden, outgoing = hidden_dispatch(block, mixer_parts, x_rows, routes_t)
    arriving = exchange(outgoing.reshape(8, 96, 256), DP).reshape(768, 256)
    rows_own = spread(arriving)
    rows_other = swap_core(rows_own)
    active = gate_up(
        core, rows_own, rows_other, norm2_gain.reshape(1, 4096), router_row, w_gate[0], w_up[0]
    )
    down_spec = pl.BlockSpec((768, 512), lambda i, t: (0, t[0] * 4 + i))
    far_down = swap_core(half_product(away, active, w_down[0], down_spec))
    down_parts = exchange(half_product(core, active, w_down[0], down_spec, far_down), CHIPS)
    back = exchange(sum_parts(down_parts).reshape(8, 96, 256), DP).reshape(768, 256)
    out_own = spread(combine(hidden, back, routes_t))
    out_other = swap_core(out_own)
    return (assemble(core, out_own, out_other), final)


def solution(mesh):
    wide = Mesh(mesh.devices.reshape(4, 2, 2, 4, 2), ("z", "ylo", "yhi", "x", "core"))
    return jax.shard_map(
        per_device,
        mesh=wide,
        in_specs=(
            P(DP, None),
            P(DP),
            P(DP, None),
            P(DP, None, TENSOR),
            P(DP, None, TENSOR),
            P(),
            P(DP, TENSOR),
            P(DP, TENSOR),
            P(None, TENSOR),
            P(TENSOR),
            P(TENSOR, None),
            P(TENSOR, None),
            P(None, TENSOR),
            P(TENSOR),
            P(None, TENSOR),
            P(TENSOR),
            P(TENSOR, DP),
            P(),
            P(),
            P(DP, None, TENSOR),
            P(DP, None, TENSOR),
            P(DP, TENSOR, None),
        ),
        out_specs=(P(DP, None), P(DP, None, TENSOR)),
        check_vma=False,
    )
```

time: 1010 us -> 381 us (0.38)
  waiting for transfers between devices: 459 us -> 108 us
  local copies, waits for them, and re-layouts: 217 us -> 14.6 us
  other arithmetic: 103 us -> 2.95 us
  Pallas kernels: 0 us -> 43.7 us
  matrix products: 43.6 us -> 0 us
  starting transfers between devices: 14 us -> 35 us
  blocking collectives: 146 us -> 161 us
    psum x2 -> x0, waiting for transfers between devices: 297 us -> none  [the longest x1 155 us: per_device(): lax.psum(partial_value_sum.astype(jnp.float32).astype(jnp.bfloat16), 'ten...]
    while x256 -> x0, local copies, waits for them, and re-layouts: 112 us -> none
    all_gather x3 -> x1, waiting for transfers between devices: 89.8 us -> 0.01 us  [per_device(): lax.all_gather(out_w, DP, axis=0, tiled=True).reshape(8, 512, 512)]
    all_to_all x1 -> x7, blocking collectives: 74.6 us -> 161 us  [exchange(): return lax.all_to_all(value, axes, split_axis=0, concat_axis=0, tiled=True)]
    psum x1 -> x0, blocking collectives: 71.2 us -> none  [per_device(): low_sum, bc_sum = lax.psum((low_part, gain_part), 'tensor')]
    reduce_sum x45 -> x1, other arithmetic: 45.2 us -> 0.03 us  [per_device(): jnp.sum(exchange(low_pair.reshape(8, 16, 640), CHIPS).astype(F32), axis=0)]
    pallas_call x0 -> x14, Pallas kernels: none -> 43.7 us  [the longest x1 16 us: gate_up(): call(body, (core,), (4,), [pl.BlockSpec((4, 768, 256), lambda i, c: (jnp....]
    dot_general x12 -> x0, matrix products: 43.6 us -> none  [the longest x1 9.92 us: per_device(): jnp.dot(active, w_down[0], preferred_element_type=jnp.float32)]
  transfers between devices with their start and end apart: 6 -> 12, of which waited for: 4 -> 10; matrix products, arithmetic and copies ran while one was open for 23% -> 1% of each run, Pallas kernels for 0% -> 3%
where the time goes in v1:
time: 381 us; the launch traced here: 380 us
  blocking collectives  161 us (42%)
  waiting for transfers between devices  108 us (28%)
  Pallas kernels  43.7 us (11%)
  starting transfers between devices  35 us (9%)
  local copies, waits for them, and re-layouts  14.6 us (4%)
  between operations  14.4 us (4%)
    all_to_all x7, blocking collectives, exchange(): return lax.all_to_all(value, axes, split_axis=0, concat_axis=0, tiled=True)  161 us
    all_to_all x4, waiting for transfers between devices, exchange(): return lax.all_to_all(value, axes, split_axis=0, concat_axis=0, tiled=True)  89.6 us
    ppermute x7, starting transfers between devices, swap_core(): return lax.ppermute(value, 'core', [(0, 1), (1, 0)])  20.1 us
    ppermute x7, waiting for transfers between devices, swap_core(): return lax.ppermute(value, 'core', [(0, 1), (1, 0)])  17.7 us
    pallas_call x1, Pallas kernels, gate_up(): call(body, (core,), (4,), [pl.BlockSpec((4, 768, 256), lambda i, c: (jnp....  16 us
    all_to_all x4, starting transfers between devices, exchange(): return lax.all_to_all(value, axes, split_axis=0, concat_axis=0, tiled=True)  14.9 us
    pallas_call x4, Pallas kernels, half_product(): call(body, (target,), (4,), [pl.BlockSpec((row_count, depth), lambda i, t...  14.2 us
    unnamed x56, local copies, waits for them, and re-layouts  13.6 us
  transfers between devices with their start and end apart: 12, of which 10 were waited for; matrix products, arithmetic and copies ran while one was open for 1% of the time, Pallas kernels for 3%

profile of v1, /device:TPU:1, one launch (start us, length us, event | category | flops | bytes accessed | tf_op | source)
XLA Modules:
  0.0 380.1 jit_solution(8485741058632535499)
XLA Ops:
  10.8 27.8 %all_to_all.55.own_ref = bf16[8,128,512]{2,1,0:T(8,128)(2,1)S(1)} all-to-all(bf16[8,128,512]{2,1,0:T(8,128)(2,1)S(1)} %shard_map.221), channel_id=1, replica_groups=mesh['z'=4,'ylo'=2,'yhi'=2,'x'=4,'core'=2] {'z','ylo'}, dimensions={0} | all-to-all | bytes 2097152 | tf_op jit(solution)/shard_map/all_to_all | solution.py:36
  38.6 4.7 %collective-permute-start = (bf16[8,128,512]{2,1,0:T(8,128)(2,1)S(1)}, bf16[8,128,512]{2,1,0:T(8,128)(2,1)S(1)}, u32[]{:S(2)}, u32[]{:S(2)}) collective-permute-start(bf16[8,128,512]{2,1,0:T(8,128)(2,1)S(1)} %all_to_all.55.own_ref), channel_id=1, source_target_pairs={{0,1},{1,0},{2,3},{3,2},{4,5},{5,4},{6,7},{7,6},{8,9},{9,8},{10,11... | collective-permute-start | bytes 3145736 | tf_op jit(solution)/shard_map/ppermute | solution.py:44
  43.3 2.3 collective-permute-done.other_ref
  49.4 3.7 all-to-all-start.1
  53.4 2.0 maximum_maximum_fusion.w_ref
  55.4 47.3 %all-to-all-done.1.parts_ref = bf16[8,2,128,512]{3,2,1,0:T(8,128)(2,1)S(1)} async-done(((bf16[8,2,128,512]{3,2,1,0:T(8,128)(2,1)}), bf16[8,2,128,512]{3,2,1,0:T(8,128)(2,1)S(1)}, u32[]{:S(2)}, u32[]{:S(2)}) %all-to-all-start.1) | async-done | bytes 2097184 | tf_op jit(solution)/shard_map/all_to_all | solution.py:36
  107.5 13.5 %all_to_all.56 = bf16[8,16,640]{2,1,0:T(8,128)(2,1)S(1)} all-to-all(bf16[8,16,640]{2,1,0:T(8,128)(2,1)S(1)} %bitcast.49), channel_id=1, replica_groups=mesh['z'=4,'ylo'=2,'yhi'=2,'x'=4,'core'=2] {'yhi','x'}, dimensions={0} | all-to-all | bytes 327680 | tf_op jit(solution)/shard_map/all_to_all | solution.py:36
  121.8 3.4 all-to-all-start.3
  128.0 4.2 %all-to-all-done.3 = bf16[8,16,640]{2,1,0:T(8,128)(2,1)S(1)} async-done(((bf16[8,16,640]{2,1,0:T(8,128)(2,1)}), bf16[8,16,640]{2,1,0:T(8,128)(2,1)S(1)}, u32[]{:S(2)}, u32[]{:S(2)}) %all-to-all-start.3) | async-done | bytes 163872 | tf_op jit(solution)/shard_map/all_to_all | solution.py:36
  132.2 3.6 all-to-all-start.4
  135.8 3.1 collective-permute-start.2
  138.9 20.7 %all-to-all-done.4.z_ref = bf16[8,2,128,512]{3,2,1,0:T(8,128)(2,1)S(1)} async-done(((bf16[8,2,128,512]{3,2,1,0:T(8,128)(2,1)}), bf16[8,2,128,512]{3,2,1,0:T(8,128)(2,1)S(1)}, u32[]{:S(2)}, u32[]{:S(2)}) %all-to-all-start.4) | async-done | bytes 2097184 | tf_op jit(solution)/shard_map/all_to_all | solution.py:36
  161.2 5.3 %shard_map.225 = (bf16[2,128,512]{2,1,0:T(8,128)(2,1)S(1)}, f32[2,16,512]{2,1,0:T(8,128)}) custom-call(s32[1]{0:T(128)} %bitcast.core_ref.target_ref, s32[2]{0:T(128)S(1)} %copy-done.23, bf16[128,640]{1,0:T(8,128)(2,1)S(1)} %bitcast.35, bf16[128,640]{1,0:T(8,128)(2,1)S(1)} %copy-done.13, bf16[8,2,128,512]{3,2,1,0:T(8,128)(2,1)S(1)} %all-to-all-done.4.z_ref, ...), custom_call_target="tpu_custom_call" | custom-call | tf_op jit(solution)/shard_map/pallas_call | solution.py:220
  166.5 2.2 copy-done
  169.9 4.2 %collective-permute-start.3 = (bf16[8,256,256]{2,1,0:T(8,128)(2,1)S(1)}, bf16[8,256,256]{2,1,0:T(8,128)(2,1)S(1)}, u32[]{:S(2)}, u32[]{:S(2)}) collective-permute-start(bf16[8,256,256]{2,1,0:T(8,128)(2,1)S(1)} %shard_map.226), channel_id=1, source_target_pairs={{0,1},{1,0},{2,3},{3,2},{4,5},{5,4},{6,7},{7,6},{8,9},{9,8},{10,11... | collective-permute-start | bytes 3145736 | tf_op jit(solution)/shard_map/ppermute | solution.py:44
  174.0 2.3 collective-permute-done.3.refs_0_
  176.3 3.1 shard_map.227
  180.4 4.2 %all-to-all-start.5 = ((bf16[8,256,256]{2,1,0:T(8,128)(2,1)}), bf16[8,256,256]{2,1,0:T(8,128)(2,1)S(1)}, u32[]{:S(2)}, u32[]{:S(2)}) async-start(bf16[8,256,256]{2,1,0:T(8,128)(2,1)} %copy-done.5), calls=%async_computation.5 | async-start | bytes 2097152 | tf_op jit(solution)/shard_map/all_to_all | solution.py:36
  184.6 17.4 %all-to-all-done.5.parts_ref = bf16[8,256,256]{2,1,0:T(8,128)(2,1)S(1)} async-done(((bf16[8,256,256]{2,1,0:T(8,128)(2,1)}), bf16[8,256,256]{2,1,0:T(8,128)(2,1)S(1)}, u32[]{:S(2)}, u32[]{:S(2)}) %all-to-all-start.5) | async-done | bytes 1048608 | tf_op jit(solution)/shard_map/all_to_all | solution.py:36
  202.4 10.2 %all_to_all.57 = bf16[8,96,256]{2,1,0:T(8,128)(2,1)S(1)} all-to-all(bf16[8,96,256]{2,1,0:T(8,128)(2,1)S(1)} %bitcast.36), channel_id=1, replica_groups=mesh['z'=4,'ylo'=2,'yhi'=2,'x'=4,'core'=2] {'z','ylo'}, dimensions={0} | all-to-all | bytes 786432 | tf_op jit(solution)/shard_map/all_to_all | solution.py:36
  212.8 40.0 %all_to_all.58.own_ref = bf16[8,768,256]{2,1,0:T(8,128)(2,1)S(1)} all-to-all(bf16[8,768,256]{2,1,0:T(8,128)(2,1)S(1)} %broadcast_in_dim.25), channel_id=1, replica_groups=mesh['z'=4,'ylo'=2,'yhi'=2,'x'=4,'core'=2] {'yhi','x'}, dimensions={0} | all-to-all | bytes 6291456 | tf_op jit(solution)/shard_map/all_to_all | solution.py:36
  252.8 3.1 collective-permute-start.4
  256.8 4.6 %collective-permute-done.4.other_ref = bf16[8,768,256]{2,1,0:T(8,128)(2,1)} collective-permute-done((bf16[8,768,256]{2,1,0:T(8,128)(2,1)S(1)}, bf16[8,768,256]{2,1,0:T(8,128)(2,1)}, u32[]{:S(2)}, u32[]{:S(2)}) %collective-permute-start.4) | collective-permute-done | bytes 3145760 | tf_op jit(solution)/shard_map/ppermute | solution.py:44
  261.3 16.0 %shard_map.229.rows_ref = bf16[768,768]{1,0:T(8,128)(2,1)S(1)} custom-call(s32[1]{0:T(128)} %bitcast.core_ref.target_ref, bf16[8,768,256]{2,1,0:T(8,128)(2,1)S(1)} %all_to_all.58.own_ref, bf16[8,768,256]{2,1,0:T(8,128)(2,1)} %collective-permute-done.4.other_ref, f32[1,4096]{1,0:T(1,128)S(1)} %bitcast.38, f32[1,4096]{1,0:T(1,128)S(1)} %bitcast_convert_fusion.router_ref, ...), custom_call_target="tpu_custom_call" | custom-call | tf_op jit(solution)/shard_map/pallas_call | solution.py:376
  277.3 4.7 %shard_map.230 = bf16[8,768,256]{2,1,0:T(8,128)(2,1)S(1)} custom-call(s32[1]{0:T(128)} %bitcast.12.target_ref, bf16[768,768]{1,0:T(8,128)(2,1)S(1)} %shard_map.229.rows_ref, bf16[768,4096]{1,0:T(8,128)(2,1)} %bitcast.44), custom_call_target="tpu_custom_call" | custom-call | tf_op jit(solution)/shard_map/pallas_call | solution.py:265
  282.5 5.3 %collective-permute-done.5.refs_0_ = bf16[8,768,256]{2,1,0:T(8,128)(2,1)S(1)} collective-permute-done((bf16[8,768,256]{2,1,0:T(8,128)(2,1)S(1)}, bf16[8,768,256]{2,1,0:T(8,128)(2,1)S(1)}, u32[]{:S(2)}, u32[]{:S(2)}) %collective-permute-start.5) | collective-permute-done | bytes 3145760 | tf_op jit(solution)/shard_map/ppermute | solution.py:44
  289.4 5.2 %shard_map.231 = bf16[8,768,256]{2,1,0:T(8,128)(2,1)S(1)} custom-call(s32[1]{0:T(128)} %bitcast.core_ref.target_ref, bf16[768,768]{1,0:T(8,128)(2,1)S(1)} %shard_map.229.rows_ref, bf16[768,4096]{1,0:T(8,128)(2,1)} %bitcast.45, bf16[8,768,256]{2,1,0:T(8,128)(2,1)} %copy-done.24), custom_call_target="tpu_custom_call" | custom-call | tf_op jit(solution)/shard_map/pallas_call | solution.py:265
  294.6 41.8 %all_to_all.59.parts_ref = bf16[8,768,256]{2,1,0:T(8,128)(2,1)S(1)} all-to-all(bf16[8,768,256]{2,1,0:T(8,128)(2,1)S(1)} %shard_map.231), channel_id=1, replica_groups=mesh['z'=4,'ylo'=2,'yhi'=2,'x'=4,'core'=2] {'yhi','x'}, dimensions={0} | all-to-all | bytes 6291456 | tf_op jit(solution)/shard_map/all_to_all | solution.py:36
  337.1 10.5 %all_to_all.60 = bf16[8,96,256]{2,1,0:T(8,128)(2,1)S(1)} all-to-all(bf16[8,96,256]{2,1,0:T(8,128)(2,1)S(1)} %bitcast.31), channel_id=1, replica_groups=mesh['z'=4,'ylo'=2,'yhi'=2,'x'=4,'core'=2] {'z','ylo'}, dimensions={0} | all-to-all | bytes 786432 | tf_op jit(solution)/shard_map/all_to_all | solution.py:36
  348.2 17.6 %all_to_all.61.own_ref = bf16[8,256,256]{2,1,0:T(8,128)(2,1)S(1)} all-to-all(bf16[8,256,256]{2,1,0:T(8,128)(2,1)S(1)} %broadcast_in_dim.26), channel_id=1, replica_groups=mesh['z'=4,'ylo'=2,'yhi'=2,'x'=4,'core'=2] {'yhi','x'}, dimensions={0} | all-to-all | bytes 2097152 | tf_op jit(solution)/shard_map/all_to_all | solution.py:36
  365.8 3.2 collective-permute-start.6
  369.1 2.3 collective-permute-done.6.other_ref
  (81 shorter events, 26.4 us)
Async XLA Ops:
  7.2 159.3 %all-gather.2.cloned.1.call-start = ((), (), s32[]{:S(2)}) async-start(), calls=%async_computation.11 | async-start | bytes 4718592 | tf_op jit(solution)/shard_map/all_gather | solution.py:490
  7.9 1.6 copy-start.1
  10.2 35.4 %copy-start.9 = (bf16[512,512]{1,0:T(8,128)(2,1)S(1)}, bf16[512,512]{1,0:T(8,128)(2,1)}, u32[]{:S(2)}) copy-start(bf16[512,512]{1,0:T(8,128)(2,1)} %w_ref.2) | copy-start | bytes 1572868
  38.6 7.0 %collective-permute-start = (bf16[8,128,512]{2,1,0:T(8,128)(2,1)S(1)}, bf16[8,128,512]{2,1,0:T(8,128)(2,1)S(1)}, u32[]{:S(2)}, u32[]{:S(2)}) collective-permute-start(bf16[8,128,512]{2,1,0:T(8,128)(2,1)S(1)} %all_to_all.55.own_ref), channel_id=1, source_target_pairs={{0,1},{1,0},{2,3},{3,2},{4,5},{5,4},{6,7},{7,6},{8,9},{9,8},{10,11... | collective-permute-start | bytes 3145736 | tf_op jit(solution)/shard_map/ppermute | solution.py:44
  47.1 1.3 copy-start.4
  49.4 3.8 copy-start.26
  49.4 3.8 copy-start.25
  49.4 53.4 %copy-start.18 = (f32[4,512]{1,0:T(4,128)S(1)}, f32[4,512]{1,0:T(4,128)}, u32[]{:S(2)}) copy-start(f32[4,512]{1,0:T(4,128)} %cw_ref.1) | copy-start | bytes 24580
  49.4 53.4 %copy-start.22 = (f32[512]{0:T(512)S(1)}, f32[512]{0:T(512)}, u32[]{:S(2)}) copy-start(f32[512]{0:T(512)} %param.31) | copy-start | bytes 6148
  49.4 53.3 %all-to-all-start.1 = ((bf16[8,2,128,512]{3,2,1,0:T(8,128)(2,1)}), bf16[8,2,128,512]{3,2,1,0:T(8,128)(2,1)S(1)}, u32[]{:S(2)}, u32[]{:S(2)}) async-start(bf16[8,2,128,512]{3,2,1,0:T(8,128)(2,1)} %copy-done.4), calls=%async_computation.1 | async-start | bytes 4194304 | tf_op jit(solution)/shard_map/all_to_all | solution.py:36
  105.1 20.0 %copy-start.7 = (bf16[8,128,512]{2,1,0:T(8,128)(2,1)S(1)}, bf16[8,128,512]{2,1,0:T(8,128)(2,1)}, u32[]{:S(2)}) copy-start(bf16[8,128,512]{2,1,0:T(8,128)(2,1)} %copy-done.6) | copy-start | bytes 3145732
  105.1 20.0 %copy-start.10 = (bf16[512,512]{1,0:T(8,128)(2,1)S(1)}, bf16[512,512]{1,0:T(8,128)(2,1)}, u32[]{:S(2)}) copy-start(bf16[512,512]{1,0:T(8,128)(2,1)} %w_ref.3) | copy-start | bytes 1572868
  105.2 2.3 collective-permute-start.1
  121.8 10.4 %all-to-all-start.3 = ((bf16[8,16,640]{2,1,0:T(8,128)(2,1)}), bf16[8,16,640]{2,1,0:T(8,128)(2,1)S(1)}, u32[]{:S(2)}, u32[]{:S(2)}) async-start(bf16[8,16,640]{2,1,0:T(8,128)(2,1)} %broadcast_in_dim.11), calls=%async_computation.3 | async-start | bytes 327680 | tf_op jit(solution)/shard_map/all_to_all | solution.py:36
  128.0 32.3 %copy-start.11 = (bf16[512,512]{1,0:T(8,128)(2,1)S(1)}, bf16[512,512]{1,0:T(8,128)(2,1)}, u32[]{:S(2)}) copy-start(bf16[512,512]{1,0:T(8,128)(2,1)} %dtp_ref.1) | copy-start | bytes 1572868
  128.0 32.3 %copy-start.14 = (f32[2,16,512]{2,1,0:T(8,128)S(1)}, f32[2,16,512]{2,1,0:T(8,128)}, u32[]{:S(2)}) copy-start(f32[2,16,512]{2,1,0:T(8,128)} %state_ref.1) | copy-start | bytes 196612
  128.0 32.3 %copy-start.15 = (f32[16,512]{1,0:T(8,128)S(1)}, f32[16,512]{1,0:T(8,128)}, u32[]{:S(2)}) copy-start(f32[16,512]{1,0:T(8,128)} %decay_ref.1) | copy-start | bytes 98308
  128.0 32.3 %copy-start.20 = (f32[512]{0:T(512)S(1)}, f32[512]{0:T(512)}, u32[]{:S(2)}) copy-start(f32[512]{0:T(512)} %param.35) | copy-start | bytes 6148
  128.0 32.3 %copy-start.21 = (f32[512]{0:T(512)S(1)}, f32[512]{0:T(512)}, u32[]{:S(2)}) copy-start(f32[512]{0:T(512)} %param.37) | copy-start | bytes 6148
  128.0 32.3 %copy-start.23 = (s32[2]{0:T(128)S(1)}, s32[2]{0:T(128)}, u32[]{:S(2)}) copy-start(s32[2]{0:T(128)} %len_ref.1) | copy-start | bytes 28
  132.2 27.4 %all-to-all-start.4 = ((bf16[8,2,128,512]{3,2,1,0:T(8,128)(2,1)}), bf16[8,2,128,512]{3,2,1,0:T(8,128)(2,1)S(1)}, u32[]{:S(2)}, u32[]{:S(2)}) async-start(bf16[8,2,128,512]{3,2,1,0:T(8,128)(2,1)} %copy-done.3), calls=%async_computation.4 | async-start | bytes 4194304 | tf_op jit(solution)/shard_map/all_to_all | solution.py:36
  135.8 23.8 %collective-permute-start.2 = (bf16[128,640]{1,0:T(8,128)(2,1)S(1)}, bf16[128,640]{1,0:T(8,128)(2,1)S(1)}, u32[]{:S(2)}, u32[]{:S(2)}) collective-permute-start(bf16[128,640]{1,0:T(8,128)(2,1)S(1)} %bitcast.34), channel_id=1, source_target_pairs={{0,1},{1,0},{2,3},{3,2},{4,5},{5,4},{6,7},{7,6},{8,9},{9,8},{10,11... | collective-permute-start | bytes 491528 | tf_op jit(solution)/shard_map/ppermute | solution.py:44
  166.5 2.2 copy-start
  169.9 6.4 %collective-permute-start.3 = (bf16[8,256,256]{2,1,0:T(8,128)(2,1)S(1)}, bf16[8,256,256]{2,1,0:T(8,128)(2,1)S(1)}, u32[]{:S(2)}, u32[]{:S(2)}) collective-permute-start(bf16[8,256,256]{2,1,0:T(8,128)(2,1)S(1)} %shard_map.226), channel_id=1, source_target_pairs={{0,1},{1,0},{2,3},{3,2},{4,5},{5,4},{6,7},{7,6},{8,9},{9,8},{10,11... | collective-permute-start | bytes 3145736 | tf_op jit(solution)/shard_map/ppermute | solution.py:44
  180.4 21.6 %copy-start.2 = (bf16[256,4096]{1,0:T(8,128)(2,1)S(1)}, bf16[256,4096]{1,0:T(8,128)(2,1)}, u32[]{:S(2)}) copy-start(bf16[256,4096]{1,0:T(8,128)(2,1)} %x_ref.3) | copy-start | bytes 6291460
  180.4 21.6 %copy-start.19 = (s32[256,2]{0,1:T(2,128)S(1)}, s32[256,2]{0,1:T(2,128)}, u32[]{:S(2)}) copy-start(s32[256,2]{0,1:T(2,128)} %param.24) | copy-start | bytes 6148
  180.4 21.6 %all-to-all-start.5 = ((bf16[8,256,256]{2,1,0:T(8,128)(2,1)}), bf16[8,256,256]{2,1,0:T(8,128)(2,1)S(1)}, u32[]{:S(2)}, u32[]{:S(2)}) async-start(bf16[8,256,256]{2,1,0:T(8,128)(2,1)} %copy-done.5), calls=%async_computation.5 | async-start | bytes 2097152 | tf_op jit(solution)/shard_map/all_to_all | solution.py:36
  212.8 48.6 %copy-start.17 = (f32[4096]{0:T(1024)S(1)}, f32[4096]{0:T(1024)}, u32[]{:S(2)}) copy-start(f32[4096]{0:T(1024)} %param.39) | copy-start | bytes 49156
  252.8 8.6 %collective-permute-start.4 = (bf16[8,768,256]{2,1,0:T(8,128)(2,1)S(1)}, bf16[8,768,256]{2,1,0:T(8,128)(2,1)}, u32[]{:S(2)}, u32[]{:S(2)}) collective-permute-start(bf16[8,768,256]{2,1,0:T(8,128)(2,1)S(1)} %all_to_all.58.own_ref), channel_id=1, source_target_pairs={{0,1},{1,0},{2,3},{3,2},{4,5},{5,4},{6,7},{7,6},{8,9},{9,8},{10,11... | collective-permute-start | bytes 9437192 | tf_op jit(solution)/shard_map/ppermute | solution.py:44
  282.0 5.7 %collective-permute-start.5 = (bf16[8,768,256]{2,1,0:T(8,128)(2,1)S(1)}, bf16[8,768,256]{2,1,0:T(8,128)(2,1)S(1)}, u32[]{:S(2)}, u32[]{:S(2)}) collective-permute-start(bf16[8,768,256]{2,1,0:T(8,128)(2,1)S(1)} %shard_map.230), channel_id=1, source_target_pairs={{0,1},{1,0},{2,3},{3,2},{4,5},{5,4},{6,7},{7,6},{8,9},{9,8},{10,11... | collective-permute-start | bytes 9437192 | tf_op jit(solution)/shard_map/ppermute | solution.py:44
  287.7 1.7 copy-start.24
  365.8 5.5 %collective-permute-start.6 = (bf16[8,256,256]{2,1,0:T(8,128)(2,1)S(1)}, bf16[8,256,256]{2,1,0:T(8,128)(2,1)S(1)}, u32[]{:S(2)}, u32[]{:S(2)}) collective-permute-start(bf16[8,256,256]{2,1,0:T(8,128)(2,1)S(1)} %all_to_all.61.own_ref), channel_id=1, source_target_pairs={{0,1},{1,0},{2,3},{3,2},{4,5},{5,4},{6,7},{7,6},{8,9},{9,8},{10,11... | collective-permute-start | bytes 3145736 | tf_op jit(solution)/shard_map/ppermute | solution.py:44
  (7 other events, 6.7 us)
Sparse Core Ops, SparseCore 0:
  9.6 127.9 all-gather.1

commit v2 on v1

--- a/solution.py
+++ b/solution.py
@@ -52,51 +52,125 @@
     return value * sigmoid(value)
 
 
-def norm_split(core, x_rows, gain):
-    def body(core_ref, x_ref, gain_ref, out_ref):
-        values = x_ref[...].astype(F32)
-        scale = lax.rsqrt(jnp.mean(values * values, axis=-1, keepdims=True) + EPS)
-        normed = (values * scale * gain_ref[...]).astype(BF16)
-        for piece in range(8):
-            out_ref[piece] = normed[:, piece * 512 : piece * 512 + 512]
-
-    return call(
-        body,
-        (core,),
+RING = (0, 3, 1, 2)
+
+
+def from_below(value):
+    return lax.ppermute(value, "z", [(i, (i + 1) % 4) for i in range(4)])
+
+
+def from_above(value):
+    return lax.ppermute(value, "z", [(i, (i - 1) % 4) for i in range(4)])
+
+
+def after(value, *earlier):
+    return lax.optimization_barrier((value,) + earlier)[0]
+
+
+def swap_pair(value):
+    return lax.ppermute(value, "ylo", [(0, 1), (1, 0)])
+
+
+def gather_ring(block, below, above, halves):
+    return block, below, above, from_below(halves[0]), from_above(halves[1])
+
+
+def second_round(below, above, pair):
+    return (
+        jnp.concatenate([below[:256], pair[:256]]),
+        jnp.concatenate([above[256:], pair[256:]]),
+        jnp.concatenate([above[:256], below[256:]]),
+    )
+
+
+def third_round(first, second, third):
+    return (
+        from_below(first[256:384]),
+        from_above(third[128:256]),
+        swap_pair(second[:256]),
+    )
+
+
+def norm_split(place, x_rows, gain):
+    def body(place_ref, x_ref, gain_ref, own_ref, send_ref):
+        request = pl.ds(pl.multiple_of(place_ref[0] * 128, 128), 128)
+        for rows, out_ref, member in (
+            (slice(0, 256), own_ref, place_ref[2]),
+            (request, send_ref, 1 - place_ref[2]),
+        ):
+            values = x_ref[rows, :].astype(F32)
+            scale = lax.rsqrt(jnp.mean(values * values, axis=-1, keepdims=True) + EPS)
+            for piece, shift in enumerate(RING):
+                at = ((place_ref[1] + shift) % 4) * 2 + member
+                columns = pl.ds(pl.multiple_of(at * 512, 512), 512)
+                part = x_ref[rows, columns].astype(F32)
+                out_ref[piece] = (part * scale * gain_ref[:, columns]).astype(BF16)
+
+    return call(
+        body,
+        (place,),
         (1,),
         [
-            pl.BlockSpec((128, 4096), lambda i, c: (c[0], 0)),
+            pl.BlockSpec((256, 4096), lambda i, c: (0, 0)),
             pl.BlockSpec((1, 4096), lambda i, c: (0, 0)),
         ],
-        pl.BlockSpec((8, 128, 512), lambda i, c: (0, 0, 0)),
-        jax.ShapeDtypeStruct((8, 128, 512), BF16),
-    )(core, x_rows, gain)
-
-
-def partial_product(own, other, weight):
-    def body(own_ref, other_ref, w_ref, out_ref):
-        weight_now = w_ref[...]
+        [
+            pl.BlockSpec((4, 256, 512), lambda i, c: (0, 0, 0)),
+            pl.BlockSpec((4, 128, 512), lambda i, c: (0, 0, 0)),
+        ],
+        [
+            jax.ShapeDtypeStruct((4, 256, 512), BF16),
+            jax.ShapeDtypeStruct((4, 128, 512), BF16),
+        ],
+    )(place, x_rows, gain)
+
+
+def ring_product(rows_ref, blocks):
+    total = None
+    for piece in range(3):
+        term = jnp.dot(rows_ref[piece], blocks[piece][...], preferred_element_type=F32)
+        total = term if total is None else total + term
+    total = total + jnp.dot(rows_ref[3, :, 0:256], blocks[3][...], preferred_element_type=F32)
+    return total + jnp.dot(rows_ref[3, :, 256:512], blocks[4][...], preferred_element_type=F32)
+
+
+RING_SPECS = [pl.BlockSpec((512, 512), lambda *_: (0, 0))] * 3 + [
+    pl.BlockSpec((256, 512), lambda *_: (0, 0))
+] * 2
+
+
+def pair_product(place, own, other, blocks):
+    def body(place_ref, own_ref, other_ref, *refs):
         for slot, rows_ref in enumerate((own_ref, other_ref)):
-            out_ref[:, slot] = (
-                jnp.dot(rows_ref[...].reshape(512, 512), weight_now, preferred_element_type=F32)
-                .astype(BF16)
-                .reshape(4, 128, 512)
-            )
-
-    rows = pl.BlockSpec((4, 128, 512), lambda i: (i, 0, 0))
+            refs[5][place_ref[0] ^ slot] = ring_product(rows_ref, refs[:5]).astype(BF16)
+
+    return call(
+        body,
+        (place,),
+        (1,),
+        [pl.BlockSpec((4, 128, 512), lambda i, c: (0, 0, 0))] * 2 + RING_SPECS,
+        pl.BlockSpec((2, 128, 512), lambda i, c: (0, 0, 0)),
+        jax.ShapeDtypeStruct((2, 128, 512), BF16),
+    )(place, own, other, *blocks)
+
+
+def own_product(rows, blocks):
+    def body(rows_ref, *refs):
+        refs[5][...] = ring_product(rows_ref, refs[:5]).reshape(2, 128, 512)
+
     return call(
         body,
         (),
-        (2,),
-        [rows, rows, pl.BlockSpec((512, 512), lambda i: (0, 0))],
-        pl.BlockSpec((4, 2, 128, 512), lambda i: (i, 0, 0, 0)),
-        jax.ShapeDtypeStruct((8, 2, 128, 512), BF16),
-    )(own, other, weight)
-
-
-def conv_project(core, parts, history, conv_w, conv_b, weight):
-    def body(core_ref, parts_ref, hist_ref, cw_ref, cb_ref, w_ref, conv_ref, low_ref, line):
-        x_inner = jnp.sum(parts_ref[:, 0].astype(F32), axis=0).astype(BF16).astype(F32)
+        (1,),
+        [pl.BlockSpec((4, 256, 512), lambda i: (0, 0, 0))] + RING_SPECS,
+        pl.BlockSpec((2, 128, 512), lambda i: (0, 0, 0)),
+        jax.ShapeDtypeStruct((2, 128, 512), F32),
+    )(rows, *blocks)
+
+
+def conv_project(core, near, far, history, conv_w, conv_b, weight):
+    def body(core_ref, near_ref, far_ref, hist_ref, cw_ref, cb_ref, w_ref, conv_ref, low_ref, line):
+        x_inner = (near_ref[0] + far_ref[0].astype(F32)).astype(BF16).astype(F32)
         line[0:8] = hist_ref[0]
         line[8:136] = x_inner
         total = cb_ref[...] + cw_ref[3:4] * x_inner
@@ -111,7 +185,8 @@
         (core,),
         (2,),
         [
-            pl.BlockSpec((8, 1, 128, 512), lambda r, c: (0, r ^ c[0], 0, 0)),
+            pl.BlockSpec((1, 128, 512), lambda r, c: (r, 0, 0)),
+            pl.BlockSpec((1, 128, 512), lambda r, c: (r, 0, 0)),
             pl.BlockSpec((1, 8, 512), lambda r, c: (r, 0, 0)),
             pl.BlockSpec((4, 512), lambda r, c: (0, 0)),
             pl.BlockSpec((1, 512), lambda r, c: (0, 0)),
@@ -126,16 +201,19 @@
             jax.ShapeDtypeStruct((2, 128, 640), BF16),
         ],
         (pltpu.VMEM((136, 512), F32),),
-    )(core, parts, history, conv_w, conv_b, weight)
-
-
-def scan_gate(core, lengths, low_own, low_other, z_parts, conv, dt_proj, dt_bias, decay, skip, state):
+    )(core, near, far, history, conv_w, conv_b, weight)
+
+
+def scan_gate(
+    core, lengths, low_own, low_other, z_near, z_far, conv, dt_proj, dt_bias, decay, skip, state
+):
     def body(
         core_ref,
         len_ref,
         own_ref,
         other_ref,
-        z_ref,
+        zn_ref,
+        zf_ref,
         conv_ref,
         dtp_ref,
         dtb_ref,
@@ -211,7 +289,7 @@
                 )
             mask = (position < len_ref[request]).astype(F32)
             mixed = jnp.concatenate(outs, axis=0) + skip_ref[...] * conv_ref[request].astype(F32)
-            z_gate = jnp.sum(z_ref[:, slot].astype(F32), axis=0).astype(BF16).astype(F32)
+            z_gate = (zn_ref[request] + zf_ref[request].astype(F32)).astype(BF16).astype(F32)
             gated_ref[request] = (mixed * silu(z_gate) * mask).astype(BF16)
 
     def whole(*shape):
@@ -224,7 +302,8 @@
         [
             whole(128, 640),
             whole(128, 640),
-            whole(8, 2, 128, 512),
+            whole(2, 128, 512),
+            whole(2, 128, 512),
             whole(2, 128, 512),
             whole(512, 512),
             whole(1, 512),
@@ -243,7 +322,67 @@
             pltpu.VMEM((2, 2048, 512), BF16),
             pltpu.VMEM((16, 512), F32),
         ),
-    )(core, lengths, low_own, low_other, z_parts, conv, dt_proj, dt_bias, decay, skip, state)
+    )(
+        core,
+        lengths,
+        low_own,
+        low_other,
+        z_near,
+        z_far,
+        conv,
+        dt_proj,
+        dt_bias,
+        decay,
+        skip,
+        state,
+    )
+
+
+def mixer_product(place, gated, blocks):
+    def body(place_ref, rows_ref, *refs):
+        own, below, above, pair, first, second, third, low, mid, high = refs[:10]
+        own_ref, other_ref = refs[10:]
+
+        def times(begin, end, ref, at):
+            return jnp.dot(
+                rows_ref[:, begin:end], ref[at : at + end - begin], preferred_element_type=F32
+            )
+
+        sums = (
+            lambda: times(0, 512, own, 0),
+            lambda: times(0, 512, below, 0),
+            lambda: times(0, 512, above, 0),
+            lambda: times(0, 256, first, 0) + times(256, 512, second, 0),
+            lambda: times(0, 512, pair, 0),
+            lambda: times(0, 256, first, 256) + times(256, 512, third, 256),
+            lambda: times(0, 256, third, 0) + times(256, 512, second, 256),
+            lambda: times(0, 128, low, 0) + times(128, 256, mid, 0) + times(256, 512, high, 0),
+        )
+        for index, make in enumerate(sums):
+            value = make().astype(BF16)
+            part = ((place_ref[1] + RING[index % 4]) % 4) * 2 + (place_ref[2] ^ (index // 4))
+
+            @pl.when(part // 4 == place_ref[0])
+            def _():
+                own_ref[part % 4, 0] = value[:, 0:256]
+                own_ref[part % 4, 1] = value[:, 256:512]
+
+            @pl.when(part // 4 != place_ref[0])
+            def _():
+                other_ref[part % 4, 0] = value[:, 0:256]
+                other_ref[part % 4, 1] = value[:, 256:512]
+
+    def whole(*shape):
+        return pl.BlockSpec(shape, lambda i, c: (0,) * len(shape))
+
+    return call(
+        body,
+        (place,),
+        (1,),
+        [whole(256, 512)] + [whole(*block.shape) for block in blocks],
+        [whole(4, 2, 256, 256)] * 2,
+        [jax.ShapeDtypeStruct((4, 2, 256, 256), BF16)] * 2,
+    )(place, gated, *blocks)
 
 
 def half_product(target, rows, weight, weight_spec, received=None):
@@ -487,27 +626,60 @@
     block = (core_at * 8 + chip_at).reshape(1)
     expert_at = lax.axis_index(DP).astype(jnp.int32)
 
-    out_full = lax.all_gather(out_w, DP, axis=0, tiled=True).reshape(8, 512, 512)
+    place = jnp.stack(
+        [core_at, lax.axis_index("z").astype(jnp.int32), lax.axis_index("ylo").astype(jnp.int32)]
+    )
     low_weight = jnp.concatenate([x_dt, x_bc, jnp.zeros((512, 96), BF16)], axis=1)
     history = jnp.pad(conv_state.astype(F32), ((0, 0), (5, 0), (0, 0)))
     routes_t = routes.T
     router_row = lax.dynamic_slice(router, (0, expert_at), (4096, 1)).astype(F32).reshape(1, 4096)
 
-    own = exchange(norm_split(core, x_rows, norm1_gain.reshape(1, 4096)), DP)
-    other = swap_core(own)
-    x_parts = exchange(partial_product(own, other, in_x), DP)
-    z_parts = exchange(partial_product(own, other, in_z), DP)
-    conv, low = conv_project(core, x_parts, history, conv_w, conv_b.reshape(1, 512), low_weight)
-    low_pair = (low[0].astype(F32) + swap_core(low[1]).astype(F32)).astype(BF16)
-    low_sum = jnp.sum(exchange(low_pair.reshape(8, 16, 640), CHIPS).astype(F32), axis=0).astype(BF16)
+    rows_mine, rows_send = norm_split(place, x_rows, norm1_gain.reshape(1, 4096))
+    pair_own = swap_pair(rows_send)
+    x_below, x_above = from_below(in_x), from_above(in_x)
+    x_halves = (x_below[:256], x_above[256:])
+    x_blocks = gather_ring(in_x, x_below, x_above, x_halves)
+    pair_other = swap_core(pair_own)
+    z_block = after(in_z, pair_other, *x_halves)
+    z_below, z_above = from_below(z_block), from_above(z_block)
+    x_far = swap_pair(pair_product(place, pair_own, pair_other, x_blocks))
+    z_halves = (z_below[:256], z_above[256:])
+    z_blocks = gather_ring(z_block, z_below, z_above, z_halves)
+    x_near = after(own_product(rows_mine, x_blocks), *z_halves)
+    conv, low = conv_project(
+        core, x_near, x_far, history, conv_w, conv_b.reshape(1, 512), low_weight
+    )
+    low_far = swap_core(low[1])
+    out_block = after(out_w, low[1])
+    out_pair, out_below, out_above = (
+        swap_pair(out_block),
+        from_below(out_block),
+        from_above(out_block),
+    )
+    low_pair = (low[0].astype(F32) + low_far.astype(F32)).astype(BF16)
+    low_parts = exchange(low_pair.reshape(8, 16, 640), CHIPS)
+    low_sum = jnp.sum(low_parts.astype(F32), axis=0).astype(BF16)
+    z_send = pair_product(place, pair_own, after(pair_other, low_parts), z_blocks)
+    out_sends = second_round(
+        after(out_below, z_send), after(out_above, z_send), after(out_pair, z_send)
+    )
+    low_sum = after(low_sum, z_send, *out_sends)
+    z_far = swap_pair(z_send)
+    z_near = own_product(rows_mine, z_blocks)
+    out_seconds = (from_below(out_sends[0]), from_above(out_sends[1]), swap_pair(out_sends[2]))
     low_own = spread(low_sum).reshape(128, 640)
+    out_seconds = tuple(after(block, low_own) for block in out_seconds)
+    out_blocks = (
+        (out_block, out_below, out_above, out_pair) + out_seconds + third_round(*out_seconds)
+    )
     low_other = swap_core(low_own)
     gated, final = scan_gate(
         core,
         lengths,
         low_own,
         low_other,
-        z_parts,
+        z_near,
+        z_far,
         conv,
         dt_proj,
         dt_bias.reshape(1, 512),
@@ -516,9 +688,9 @@
         ssm_state,
     )
     gated = gated.reshape(256, 512)
-    out_spec = pl.BlockSpec((1, 512, 512), lambda i, t: (t[0] * 4 + i, 0, 0))
-    far = swap_core(half_product(away, gated, out_full, out_spec))
-    mixer_parts = exchange(half_product(core, gated, out_full, out_spec, far), CHIPS)
+    mixer_own, mixer_other = mixer_product(place, gated, out_blocks)
+    mixer_pair = (mixer_own.astype(F32) + swap_core(mixer_other).astype(F32)).astype(BF16)
+    mixer_parts = exchange(mixer_pair.reshape(8, 256, 256), CHIPS)
     hidden, outgoing = hidden_dispatch(block, mixer_parts, x_rows, routes_t)
     arriving = exchange(outgoing.reshape(8, 96, 256), DP).reshape(768, 256)
     rows_own = spread(arriving)

time: 381 us -> 316 us (0.83)
  waiting for transfers between devices: 108 us -> 55.8 us
  blocking collectives: 161 us -> 136 us
  starting transfers between devices: 35 us -> 51.4 us
  between operations: 14.4 us -> 1.2 us
  Pallas kernels: 43.7 us -> 51.6 us
  other arithmetic: 2.95 us -> 6.93 us
    all_to_all x4 -> x2, waiting for transfers between devices: 89.6 us -> 24.6 us  [exchange(): return lax.all_to_all(value, axes, split_axis=0, concat_axis=0, tiled=True)]
    all_to_all x7 -> x6, blocking collectives: 161 us -> 136 us  [exchange(): return lax.all_to_all(value, axes, split_axis=0, concat_axis=0, tiled=True)]
    ppermute x0 -> x20, starting transfers between devices: none -> 24.8 us  [the longest x7 17.4 us: from_above(): return lax.ppermute(value, 'z', [(i, (i - 1) % 4) for i in range(4)])]
    ppermute x0 -> x20, waiting for transfers between devices: none -> 16.5 us  [the longest x7 8.97 us: from_below(): return lax.ppermute(value, 'z', [(i, (i + 1) % 4) for i in range(4)])]
    pallas_call x4 -> x7, Pallas kernels: 4.75 us -> 15.8 us  [the longest x1 5.54 us: mixer_product(): call(body, (place,), (1,), [whole(256, 512)] + [whole(*block.shape) for b...]
    unnamed x56 -> x68, local copies, waits for them, and re-layouts: 13.6 us -> 7.76 us
    ppermute x7, starting transfers between devices: 20.1 us -> 15 us  [swap_core(): return lax.ppermute(value, 'core', [(0, 1), (1, 0)])]
    pallas_call x4 -> x2, Pallas kernels: 14.2 us -> 9.92 us  [half_product(): call(body, (target,), (4,), [pl.BlockSpec((row_count, depth), lambda i, t...]
  transfers between devices with their start and end apart: 12 -> 29, of which waited for: 10 -> 11; matrix products, arithmetic and copies ran while one was open for 1% -> 3% of each run, Pallas kernels for 3% -> 4%
where the time goes in v2:
time: 316 us; the launch traced here: 315 us
  blocking collectives  136 us (43%)
  waiting for transfers between devices  55.8 us (18%)
  Pallas kernels  51.6 us (16%)
  starting transfers between devices  51.4 us (16%)
  local copies, waits for them, and re-layouts  11.9 us (4%)
  other arithmetic  6.93 us (2%)
    all_to_all x6, blocking collectives, exchange(): return lax.all_to_all(value, axes, split_axis=0, concat_axis=0, tiled=True)  136 us
    all_to_all x2, waiting for transfers between devices, exchange(): return lax.all_to_all(value, axes, split_axis=0, concat_axis=0, tiled=True)  24.6 us
    ppermute x7, starting transfers between devices, from_above(): return lax.ppermute(value, 'z', [(i, (i - 1) % 4) for i in range(4)])  17.4 us
    pallas_call x1, Pallas kernels, gate_up(): call(body, (core,), (4,), [pl.BlockSpec((4, 768, 256), lambda i, c: (jnp....  16 us
    ppermute x7, starting transfers between devices, swap_core(): return lax.ppermute(value, 'core', [(0, 1), (1, 0)])  15 us
    ppermute x7, waiting for transfers between devices, swap_core(): return lax.ppermute(value, 'core', [(0, 1), (1, 0)])  14.7 us
    all_to_all x2, starting transfers between devices, exchange(): return lax.all_to_all(value, axes, split_axis=0, concat_axis=0, tiled=True)  11.6 us
    pallas_call x2, Pallas kernels, half_product(): call(body, (target,), (4,), [pl.BlockSpec((row_count, depth), lambda i, t...  9.92 us
  transfers between devices with their start and end apart: 29, of which 11 were waited for; matrix products, arithmetic and copies ran while one was open for 3% of the time, Pallas kernels for 4%

profile of v2, /device:TPU:1, one launch (start us, length us, event | category | flops | bytes accessed | tf_op | source)
XLA Modules:
  0.0 314.5 jit_solution(15809092710074576563)
XLA Ops:
  4.8 2.2 collective-permute-start.4
  10.7 7.5 %collective-permute-done.4.own_ref = bf16[4,128,512]{2,1,0:T(8,128)(2,1)S(1)} collective-permute-done((bf16[4,128,512]{2,1,0:T(8,128)(2,1)S(1)}, bf16[4,128,512]{2,1,0:T(8,128)(2,1)S(1)}, u32[]{:S(2)}, u32[]{:S(2)}) %collective-permute-start.4) | collective-permute-done | bytes 524320 | tf_op jit(solution)/shard_map/ppermute | solution.py:71
  19.9 2.2 collective-permute-done.refs_1_
  22.2 2.7 collective-permute-start.3
  24.9 2.7 collective-permute-start.7
  37.3 3.5 %collective-permute-done.6.refs_1_ = bf16[512,512]{1,0:T(8,128)(2,1)S(1)} collective-permute-done((bf16[512,512]{1,0:T(8,128)(2,1)}, bf16[512,512]{1,0:T(8,128)(2,1)S(1)}, u32[]{:S(2)}, u32[]{:S(2)}) %collective-permute-start.6) | collective-permute-done | bytes 524320 | tf_op jit(solution)/shard_map/ppermute | solution.py:59
  42.8 2.5 collective-permute-start.9
  48.5 2.7 collective-permute-start.11
  51.2 13.5 %all_to_all.40 = bf16[8,16,640]{2,1,0:T(8,128)(2,1)} all-to-all(bf16[8,16,640]{2,1,0:T(8,128)(2,1)S(1)} %bitcast.47), channel_id=1, replica_groups=mesh['z'=4,'ylo'=2,'yhi'=2,'x'=4,'core'=2] {'yhi','x'}, dimensions={0} | all-to-all | bytes 327680 | tf_op jit(solution)/shard_map/all_to_all | solution.py:36
  65.9 2.3 shard_map.225
  69.3 2.3 collective-permute-start.18
  76.0 6.4 %all-to-all-start.1 = ((bf16[8,16,640]{2,1,0:T(8,128)(2,1)}), bf16[8,16,640]{2,1,0:T(8,128)(2,1)}, u32[]{:S(2)}, u32[]{:S(2)}) async-start(bf16[8,16,640]{2,1,0:T(8,128)(2,1)} %broadcast_in_dim.11), calls=%async_computation.1 | async-start | bytes 327680 | tf_op jit(solution)/shard_map/all_to_all | solution.py:36
  82.3 7.2 %all-to-all-done.1 = bf16[8,16,640]{2,1,0:T(8,128)(2,1)} async-done(((bf16[8,16,640]{2,1,0:T(8,128)(2,1)}), bf16[8,16,640]{2,1,0:T(8,128)(2,1)}, u32[]{:S(2)}, u32[]{:S(2)}) %all-to-all-start.1) | async-done | bytes 163872 | tf_op jit(solution)/shard_map/all_to_all | solution.py:36
  90.8 4.7 %collective-permute-start.15 = (bf16[128,640]{1,0:T(8,128)(2,1)}, bf16[128,640]{1,0:T(8,128)(2,1)S(1)}, u32[]{:S(2)}, u32[]{:S(2)}) collective-permute-start(bf16[128,640]{1,0:T(8,128)(2,1)} %bitcast.9.own_ref), channel_id=1, source_target_pairs={{0,1},{1,0},{2,3},{3,2},{4,5},{5,4},{6,7},{7,6},{8,9},{9,8},{10,11... | collective-permute-start | bytes 491528 | tf_op jit(solution)/shard_map/ppermute | solution.py:44
  97.4 3.2 %collective-permute-start.21 = (bf16[128,512]{1,0:T(8,128)(2,1)S(1)}, bf16[128,512]{1,0:T(8,128)(2,1)S(1)}, u32[]{:S(2)}, u32[]{:S(2)}) collective-permute-start(bf16[128,512]{1,0:T(8,128)(2,1)S(1)} %slice.59), channel_id=1, source_target_pairs={{0,96},{32,0},{64,32},{96,64},{1,97},{33,1},{65,33},{97,65},{2,98}... | collective-permute-start | bytes 393224 | tf_op jit(solution)/shard_map/ppermute | solution.py:63
  103.4 6.3 %shard_map.227 = (bf16[2,128,512]{2,1,0:T(8,128)(2,1)S(1)}, f32[2,16,512]{2,1,0:T(8,128)}) custom-call(s32[1]{0:T(128)} %bitcast.core_ref.target_ref, s32[2]{0:T(128)S(1)} %copy-done.29, bf16[128,640]{1,0:T(8,128)(2,1)} %bitcast.9.own_ref, bf16[128,640]{1,0:T(8,128)(2,1)S(1)} %collective-permute-done.15.other_ref, f32[2,128,512]{2,1,0:T(8,128)S(1)} %shard_map.226.zn_ref, ...), custom_call_target="tpu_custom_call" | custom-call | tf_op jit(solution)/shard_map/pallas_call | solution.py:298
  109.7 5.5 %shard_map.228 = (bf16[4,2,256,256]{3,2,1,0:T(8,128)(2,1)S(1)}, bf16[4,2,256,256]{3,2,1,0:T(8,128)(2,1)}) custom-call(s32[3]{0:T(128)S(1)} %pad_add_fusion.place_ref, bf16[256,512]{1,0:T(8,128)(2,1)S(1)} %bitcast.33, bf16[512,512]{1,0:T(8,128)(2,1)S(1)} %copy-done.16, bf16[512,512]{1,0:T(8,128)(2,1)S(1)} %collective-permute-done.12.refs_1_, ...), custom_call_target="tpu_custom_call" | custom-call | tf_op jit(solution)/shard_map/pallas_call | solution.py:378
  115.6 2.6 collective-permute-done.23
  119.4 5.3 %all-to-all-start.2 = ((bf16[8,256,256]{2,1,0:T(8,128)(2,1)}), bf16[8,256,256]{2,1,0:T(8,128)(2,1)S(1)}, u32[]{:S(2)}, u32[]{:S(2)}) async-start(bf16[8,256,256]{2,1,0:T(8,128)(2,1)} %bitcast.45), calls=%async_computation.2 | async-start | bytes 2097152 | tf_op jit(solution)/shard_map/all_to_all | solution.py:36
  124.6 17.4 %all-to-all-done.2.parts_ref = bf16[8,256,256]{2,1,0:T(8,128)(2,1)S(1)} async-done(((bf16[8,256,256]{2,1,0:T(8,128)(2,1)}), bf16[8,256,256]{2,1,0:T(8,128)(2,1)S(1)}, u32[]{:S(2)}, u32[]{:S(2)}) %all-to-all-start.2) | async-done | bytes 1048608 | tf_op jit(solution)/shard_map/all_to_all | solution.py:36
  142.5 10.5 %all_to_all.41 = bf16[8,96,256]{2,1,0:T(8,128)(2,1)S(1)} all-to-all(bf16[8,96,256]{2,1,0:T(8,128)(2,1)S(1)} %bitcast.32), channel_id=1, replica_groups=mesh['z'=4,'ylo'=2,'yhi'=2,'x'=4,'core'=2] {'z','ylo'}, dimensions={0} | all-to-all | bytes 786432 | tf_op jit(solution)/shard_map/all_to_all | solution.py:36
  153.2 40.9 %all_to_all.42.own_ref = bf16[8,768,256]{2,1,0:T(8,128)(2,1)S(1)} all-to-all(bf16[8,768,256]{2,1,0:T(8,128)(2,1)S(1)} %broadcast_in_dim.25), channel_id=1, replica_groups=mesh['z'=4,'ylo'=2,'yhi'=2,'x'=4,'core'=2] {'yhi','x'}, dimensions={0} | all-to-all | bytes 6291456 | tf_op jit(solution)/shard_map/all_to_all | solution.py:36
  194.0 3.1 collective-permute-start.24
  198.0 4.6 %collective-permute-done.24.other_ref = bf16[8,768,256]{2,1,0:T(8,128)(2,1)} collective-permute-done((bf16[8,768,256]{2,1,0:T(8,128)(2,1)S(1)}, bf16[8,768,256]{2,1,0:T(8,128)(2,1)}, u32[]{:S(2)}, u32[]{:S(2)}) %collective-permute-start.24) | collective-permute-done | bytes 3145760 | tf_op jit(solution)/shard_map/ppermute | solution.py:44
  202.6 16.0 %shard_map.230.rows_ref = bf16[768,768]{1,0:T(8,128)(2,1)S(1)} custom-call(s32[1]{0:T(128)} %bitcast.core_ref.target_ref, bf16[8,768,256]{2,1,0:T(8,128)(2,1)S(1)} %all_to_all.42.own_ref, bf16[8,768,256]{2,1,0:T(8,128)(2,1)} %collective-permute-done.24.other_ref, f32[1,4096]{1,0:T(1,128)S(1)} %bitcast.35, f32[1,4096]{1,0:T(1,128)S(1)} %bitcast_convert_fusion.router_ref, ...), custom_call_target="tpu_custom_call" | custom-call | tf_op jit(solution)/shard_map/pallas_call | solution.py:515
  218.6 4.7 %shard_map.231 = bf16[8,768,256]{2,1,0:T(8,128)(2,1)S(1)} custom-call(s32[1]{0:T(128)} %bitcast.22.target_ref, bf16[768,768]{1,0:T(8,128)(2,1)S(1)} %shard_map.230.rows_ref, bf16[768,4096]{1,0:T(8,128)(2,1)} %bitcast.41), custom_call_target="tpu_custom_call" | custom-call | tf_op jit(solution)/shard_map/pallas_call | solution.py:404
  223.7 5.3 %collective-permute-done.25.refs_0_ = bf16[8,768,256]{2,1,0:T(8,128)(2,1)S(1)} collective-permute-done((bf16[8,768,256]{2,1,0:T(8,128)(2,1)S(1)}, bf16[8,768,256]{2,1,0:T(8,128)(2,1)S(1)}, u32[]{:S(2)}, u32[]{:S(2)}) %collective-permute-start.25) | collective-permute-done | bytes 3145760 | tf_op jit(solution)/shard_map/ppermute | solution.py:44
  230.7 5.2 %shard_map.232 = bf16[8,768,256]{2,1,0:T(8,128)(2,1)S(1)} custom-call(s32[1]{0:T(128)} %bitcast.core_ref.target_ref, bf16[768,768]{1,0:T(8,128)(2,1)S(1)} %shard_map.230.rows_ref, bf16[768,4096]{1,0:T(8,128)(2,1)} %bitcast.42, bf16[8,768,256]{2,1,0:T(8,128)(2,1)} %copy-done.30), custom_call_target="tpu_custom_call" | custom-call | tf_op jit(solution)/shard_map/pallas_call | solution.py:404
  235.9 42.3 %all_to_all.43.parts_ref = bf16[8,768,256]{2,1,0:T(8,128)(2,1)S(1)} all-to-all(bf16[8,768,256]{2,1,0:T(8,128)(2,1)S(1)} %shard_map.232), channel_id=1, replica_groups=mesh['z'=4,'ylo'=2,'yhi'=2,'x'=4,'core'=2] {'yhi','x'}, dimensions={0} | all-to-all | bytes 6291456 | tf_op jit(solution)/shard_map/all_to_all | solution.py:36
  278.9 10.3 %all_to_all.44 = bf16[8,96,256]{2,1,0:T(8,128)(2,1)S(1)} all-to-all(bf16[8,96,256]{2,1,0:T(8,128)(2,1)S(1)} %bitcast.31), channel_id=1, replica_groups=mesh['z'=4,'ylo'=2,'yhi'=2,'x'=4,'core'=2] {'z','ylo'}, dimensions={0} | all-to-all | bytes 786432 | tf_op jit(solution)/shard_map/all_to_all | solution.py:36
  289.8 18.4 %all_to_all.45.own_ref = bf16[8,256,256]{2,1,0:T(8,128)(2,1)S(1)} all-to-all(bf16[8,256,256]{2,1,0:T(8,128)(2,1)S(1)} %broadcast_in_dim.26), channel_id=1, replica_groups=mesh['z'=4,'ylo'=2,'yhi'=2,'x'=4,'core'=2] {'yhi','x'}, dimensions={0} | all-to-all | bytes 2097152 | tf_op jit(solution)/shard_map/all_to_all | solution.py:36
  310.3 2.3 collective-permute-done.26.other_ref
  (140 shorter events, 47.2 us)
Async XLA Ops:
  4.8 13.4 %collective-permute-start.4 = (bf16[4,128,512]{2,1,0:T(8,128)(2,1)S(1)}, bf16[4,128,512]{2,1,0:T(8,128)(2,1)S(1)}, u32[]{:S(2)}, u32[]{:S(2)}) collective-permute-start(bf16[4,128,512]{2,1,0:T(8,128)(2,1)S(1)} %get-tuple-element.24), channel_id=1, source_target_pairs={{0,16},{16,0},{1,17},{17,1},{2,18},{18,2},{3,19},{19,3},{4,20},{20... | collective-permute-start | bytes 1572872 | tf_op jit(solution)/shard_map/ppermute | solution.py:71
  7.0 15.1 %collective-permute-start = (bf16[512,512]{1,0:T(8,128)(2,1)S(1)}, bf16[512,512]{1,0:T(8,128)(2,1)S(1)}, u32[]{:S(2)}, u32[]{:S(2)}) collective-permute-start(bf16[512,512]{1,0:T(8,128)(2,1)S(1)} %copy-done.2), channel_id=1, source_target_pairs={{0,32},{32,64},{64,96},{96,0},{1,33},{33,65},{65,97},{97,1},{2,34}... | collective-permute-start | bytes 1572872 | tf_op jit(solution)/shard_map/ppermute | solution.py:59
  8.6 13.6 %collective-permute-start.1 = (bf16[512,512]{1,0:T(8,128)(2,1)S(1)}, bf16[512,512]{1,0:T(8,128)(2,1)S(1)}, u32[]{:S(2)}, u32[]{:S(2)}) collective-permute-start(bf16[512,512]{1,0:T(8,128)(2,1)S(1)} %copy-done.2), channel_id=1, source_target_pairs={{0,96},{32,0},{64,32},{96,64},{1,97},{33,1},{65,33},{97,65},{2,98}... | collective-permute-start | bytes 1572872 | tf_op jit(solution)/shard_map/ppermute | solution.py:63
  18.2 6.7 %collective-permute-start.5 = (bf16[4,128,512]{2,1,0:T(8,128)(2,1)S(1)}, bf16[4,128,512]{2,1,0:T(8,128)(2,1)S(1)}, u32[]{:S(2)}, u32[]{:S(2)}) collective-permute-start(bf16[4,128,512]{2,1,0:T(8,128)(2,1)S(1)} %collective-permute-done.4.own_ref), channel_id=1, source_target_pairs={{0,1},{1,0},{2,3},{3,2},{4,5},{5,4},{6,7},{7,6},{8,9},{9,8},{10,11... | collective-permute-start | bytes 1572872 | tf_op jit(solution)/shard_map/ppermute | solution.py:44
  22.1 7.5 %collective-permute-start.2 = (bf16[256,512]{1,0:T(8,128)(2,1)S(1)}, bf16[256,512]{1,0:T(8,128)(2,1)S(1)}, u32[]{:S(2)}, u32[]{:S(2)}) collective-permute-start(bf16[256,512]{1,0:T(8,128)(2,1)S(1)} %slice.61), channel_id=1, source_target_pairs={{0,32},{32,64},{64,96},{96,0},{1,33},{33,65},{65,97},{97,1},{2,34}... | collective-permute-start | bytes 786440 | tf_op jit(solution)/shard_map/ppermute | solution.py:59
  22.2 7.4 %collective-permute-start.3 = (bf16[256,512]{1,0:T(8,128)(2,1)S(1)}, bf16[256,512]{1,0:T(8,128)(2,1)S(1)}, u32[]{:S(2)}, u32[]{:S(2)}) collective-permute-start(bf16[256,512]{1,0:T(8,128)(2,1)S(1)} %slice.62), channel_id=1, source_target_pairs={{0,96},{32,0},{64,32},{96,64},{1,97},{33,1},{65,33},{97,65},{2,98}... | collective-permute-start | bytes 786440 | tf_op jit(solution)/shard_map/ppermute | solution.py:63
  24.9 15.9 %collective-permute-start.6 = (bf16[512,512]{1,0:T(8,128)(2,1)}, bf16[512,512]{1,0:T(8,128)(2,1)S(1)}, u32[]{:S(2)}, u32[]{:S(2)}) collective-permute-start(bf16[512,512]{1,0:T(8,128)(2,1)} %refs_0_.5), channel_id=1, source_target_pairs={{0,32},{32,64},{64,96},{96,0},{1,33},{33,65},{65,97},{97,1},{2,34}... | collective-permute-start | bytes 1572872 | tf_op jit(solution)/shard_map/ppermute | solution.py:59
  24.9 15.9 %collective-permute-start.7 = (bf16[512,512]{1,0:T(8,128)(2,1)}, bf16[512,512]{1,0:T(8,128)(2,1)S(1)}, u32[]{:S(2)}, u32[]{:S(2)}) collective-permute-start(bf16[512,512]{1,0:T(8,128)(2,1)} %refs_0_.5), channel_id=1, source_target_pairs={{0,96},{32,0},{64,32},{96,64},{1,97},{33,1},{65,33},{97,65},{2,98}... | collective-permute-start | bytes 1572872 | tf_op jit(solution)/shard_map/ppermute | solution.py:63
  31.6 9.3 %collective-permute-start.8 = (bf16[2,128,512]{2,1,0:T(8,128)(2,1)}, bf16[2,128,512]{2,1,0:T(8,128)(2,1)}, u32[]{:S(2)}, u32[]{:S(2)}) collective-permute-start(bf16[2,128,512]{2,1,0:T(8,128)(2,1)} %shard_map.223), channel_id=1, source_target_pairs={{0,16},{16,0},{1,17},{17,1},{2,18},{18,2},{3,19},{19,3},{4,20},{20... | collective-permute-start | bytes 786440 | tf_op jit(solution)/shard_map/ppermute | solution.py:71
  37.3 28.6 %copy-start.7 = (bf16[4,128,512]{2,1,0:T(8,128)(2,1)S(1)}, bf16[4,128,512]{2,1,0:T(8,128)(2,1)}, u32[]{:S(2)}) copy-start(bf16[4,128,512]{2,1,0:T(8,128)(2,1)} %copy-done.6) | copy-start | bytes 1572868
  37.3 28.6 %copy-start.9 = (bf16[4,128,512]{2,1,0:T(8,128)(2,1)S(1)}, bf16[4,128,512]{2,1,0:T(8,128)(2,1)}, u32[]{:S(2)}) copy-start(bf16[4,128,512]{2,1,0:T(8,128)(2,1)} %copy-done.8) | copy-start | bytes 1572868
  42.8 5.7 %collective-permute-start.9 = (bf16[128,640]{1,0:T(8,128)(2,1)S(1)}, bf16[128,640]{1,0:T(8,128)(2,1)S(1)}, u32[]{:S(2)}, u32[]{:S(2)}) collective-permute-start(bf16[128,640]{1,0:T(8,128)(2,1)S(1)} %slice_bitcast_fusion), channel_id=1, source_target_pairs={{0,1},{1,0},{2,3},{3,2},{4,5},{5,4},{6,7},{7,6},{8,9},{9,8},{10,11... | collective-permute-start | bytes 491528 | tf_op jit(solution)/shard_map/ppermute | solution.py:44
  45.3 22.9 %collective-permute-start.12 = (bf16[512,512]{1,0:T(8,128)(2,1)S(1)}, bf16[512,512]{1,0:T(8,128)(2,1)S(1)}, u32[]{:S(2)}, u32[]{:S(2)}) collective-permute-start(bf16[512,512]{1,0:T(8,128)(2,1)S(1)} %copy-done.15), channel_id=1, source_target_pairs={{0,32},{32,64},{64,96},{96,0},{1,33},{33,65},{65,97},{97,1},{2,34}... | collective-permute-start | bytes 1572872 | tf_op jit(solution)/shard_map/ppermute | solution.py:59
  45.4 22.8 %collective-permute-start.13 = (bf16[512,512]{1,0:T(8,128)(2,1)S(1)}, bf16[512,512]{1,0:T(8,128)(2,1)S(1)}, u32[]{:S(2)}, u32[]{:S(2)}) collective-permute-start(bf16[512,512]{1,0:T(8,128)(2,1)S(1)} %copy-done.15), channel_id=1, source_target_pairs={{0,16},{16,0},{1,17},{17,1},{2,18},{18,2},{3,19},{19,3},{4,20},{20... | collective-permute-start | bytes 1572872 | tf_op jit(solution)/shard_map/ppermute | solution.py:71
  46.7 21.5 %collective-permute-start.14 = (bf16[512,512]{1,0:T(8,128)(2,1)S(1)}, bf16[512,512]{1,0:T(8,128)(2,1)S(1)}, u32[]{:S(2)}, u32[]{:S(2)}) collective-permute-start(bf16[512,512]{1,0:T(8,128)(2,1)S(1)} %copy-done.15), channel_id=1, source_target_pairs={{0,96},{32,0},{64,32},{96,64},{1,97},{33,1},{65,33},{97,65},{2,98}... | collective-permute-start | bytes 1572872 | tf_op jit(solution)/shard_map/ppermute | solution.py:63
  48.4 17.4 %collective-permute-start.10 = (bf16[256,512]{1,0:T(8,128)(2,1)S(1)}, bf16[256,512]{1,0:T(8,128)(2,1)S(1)}, u32[]{:S(2)}, u32[]{:S(2)}) collective-permute-start(bf16[256,512]{1,0:T(8,128)(2,1)S(1)} %slice.63), channel_id=1, source_target_pairs={{0,32},{32,64},{64,96},{96,0},{1,33},{33,65},{65,97},{97,1},{2,34}... | collective-permute-start | bytes 786440 | tf_op jit(solution)/shard_map/ppermute | solution.py:59
  48.5 17.4 %collective-permute-start.11 = (bf16[256,512]{1,0:T(8,128)(2,1)S(1)}, bf16[256,512]{1,0:T(8,128)(2,1)S(1)}, u32[]{:S(2)}, u32[]{:S(2)}) collective-permute-start(bf16[256,512]{1,0:T(8,128)(2,1)S(1)} %slice.64), channel_id=1, source_target_pairs={{0,96},{32,0},{64,32},{96,64},{1,97},{33,1},{65,33},{97,65},{2,98}... | collective-permute-start | bytes 786440 | tf_op jit(solution)/shard_map/ppermute | solution.py:63
  69.3 20.3 %collective-permute-start.18 = (bf16[512,512]{1,0:T(8,128)(2,1)}, bf16[512,512]{1,0:T(8,128)(2,1)}, u32[]{:S(2)}, u32[]{:S(2)}) collective-permute-start(bf16[512,512]{1,0:T(8,128)(2,1)} %pad_maximum_fusion.1), channel_id=1, source_target_pairs={{0,96},{32,0},{64,32},{96,64},{1,97},{33,1},{65,33},{97,65},{2,98}... | collective-permute-start | bytes 1572872 | tf_op jit(solution)/shard_map/ppermute | solution.py:63
  72.4 23.0 %collective-permute-start.17 = (bf16[512,512]{1,0:T(8,128)(2,1)}, bf16[512,512]{1,0:T(8,128)(2,1)}, u32[]{:S(2)}, u32[]{:S(2)}) collective-permute-start(bf16[512,512]{1,0:T(8,128)(2,1)} %pad_maximum_fusion), channel_id=1, source_target_pairs={{0,32},{32,64},{64,96},{96,0},{1,33},{33,65},{65,97},{97,1},{2,34}... | collective-permute-start | bytes 1572872 | tf_op jit(solution)/shard_map/ppermute | solution.py:59
  73.2 22.2 %collective-permute-start.19 = (bf16[512,512]{1,0:T(8,128)(2,1)}, bf16[512,512]{1,0:T(8,128)(2,1)}, u32[]{:S(2)}, u32[]{:S(2)}) collective-permute-start(bf16[512,512]{1,0:T(8,128)(2,1)} %pad_maximum_fusion.2), channel_id=1, source_target_pairs={{0,16},{16,0},{1,17},{17,1},{2,18},{18,2},{3,19},{19,3},{4,20},{20... | collective-permute-start | bytes 1572872 | tf_op jit(solution)/shard_map/ppermute | solution.py:71
  76.0 13.6 %all-to-all-start.1 = ((bf16[8,16,640]{2,1,0:T(8,128)(2,1)}), bf16[8,16,640]{2,1,0:T(8,128)(2,1)}, u32[]{:S(2)}, u32[]{:S(2)}) async-start(bf16[8,16,640]{2,1,0:T(8,128)(2,1)} %broadcast_in_dim.11), calls=%async_computation.1 | async-start | bytes 327680 | tf_op jit(solution)/shard_map/all_to_all | solution.py:36
  82.3 21.0 %collective-permute-start.16 = (bf16[2,128,512]{2,1,0:T(8,128)(2,1)}, bf16[2,128,512]{2,1,0:T(8,128)(2,1)}, u32[]{:S(2)}, u32[]{:S(2)}) collective-permute-start(bf16[2,128,512]{2,1,0:T(8,128)(2,1)} %copy-done.19), channel_id=1, source_target_pairs={{0,16},{16,0},{1,17},{17,1},{2,18},{18,2},{3,19},{19,3},{4,20},{20... | collective-permute-start | bytes 786440 | tf_op jit(solution)/shard_map/ppermute | solution.py:71
  90.7 19.0 %collective-permute-start.22 = (bf16[256,512]{1,0:T(8,128)(2,1)S(1)}, bf16[256,512]{1,0:T(8,128)(2,1)S(1)}, u32[]{:S(2)}, u32[]{:S(2)}) collective-permute-start(bf16[256,512]{1,0:T(8,128)(2,1)S(1)} %slice.60), channel_id=1, source_target_pairs={{0,16},{16,0},{1,17},{17,1},{2,18},{18,2},{3,19},{19,3},{4,20},{20... | collective-permute-start | bytes 786440 | tf_op jit(solution)/shard_map/ppermute | solution.py:71
  90.8 12.5 %collective-permute-start.15 = (bf16[128,640]{1,0:T(8,128)(2,1)}, bf16[128,640]{1,0:T(8,128)(2,1)S(1)}, u32[]{:S(2)}, u32[]{:S(2)}) collective-permute-start(bf16[128,640]{1,0:T(8,128)(2,1)} %bitcast.9.own_ref), channel_id=1, source_target_pairs={{0,1},{1,0},{2,3},{3,2},{4,5},{5,4},{6,7},{7,6},{8,9},{9,8},{10,11... | collective-permute-start | bytes 491528 | tf_op jit(solution)/shard_map/ppermute | solution.py:44
  96.4 13.3 %collective-permute-start.20 = (bf16[128,512]{1,0:T(8,128)(2,1)S(1)}, bf16[128,512]{1,0:T(8,128)(2,1)S(1)}, u32[]{:S(2)}, u32[]{:S(2)}) collective-permute-start(bf16[128,512]{1,0:T(8,128)(2,1)S(1)} %slice.58), channel_id=1, source_target_pairs={{0,32},{32,64},{64,96},{96,0},{1,33},{33,65},{65,97},{97,1},{2,34}... | collective-permute-start | bytes 393224 | tf_op jit(solution)/shard_map/ppermute | solution.py:59
  97.4 12.3 %collective-permute-start.21 = (bf16[128,512]{1,0:T(8,128)(2,1)S(1)}, bf16[128,512]{1,0:T(8,128)(2,1)S(1)}, u32[]{:S(2)}, u32[]{:S(2)}) collective-permute-start(bf16[128,512]{1,0:T(8,128)(2,1)S(1)} %slice.59), channel_id=1, source_target_pairs={{0,96},{32,0},{64,32},{96,64},{1,97},{33,1},{65,33},{97,65},{2,98}... | collective-permute-start | bytes 393224 | tf_op jit(solution)/shard_map/ppermute | solution.py:63
  115.2 2.9 collective-permute-start.23
  119.4 22.6 %all-to-all-start.2 = ((bf16[8,256,256]{2,1,0:T(8,128)(2,1)}), bf16[8,256,256]{2,1,0:T(8,128)(2,1)S(1)}, u32[]{:S(2)}, u32[]{:S(2)}) async-start(bf16[8,256,256]{2,1,0:T(8,128)(2,1)} %bitcast.45), calls=%async_computation.2 | async-start | bytes 2097152 | tf_op jit(solution)/shard_map/all_to_all | solution.py:36
  153.1 49.4 %copy-start.23 = (f32[4096]{0:T(1024)S(1)}, f32[4096]{0:T(1024)}, u32[]{:S(2)}) copy-start(f32[4096]{0:T(1024)} %param.39) | copy-start | bytes 49156
  194.0 8.5 %collective-permute-start.24 = (bf16[8,768,256]{2,1,0:T(8,128)(2,1)S(1)}, bf16[8,768,256]{2,1,0:T(8,128)(2,1)}, u32[]{:S(2)}, u32[]{:S(2)}) collective-permute-start(bf16[8,768,256]{2,1,0:T(8,128)(2,1)S(1)} %all_to_all.42.own_ref), channel_id=1, source_target_pairs={{0,1},{1,0},{2,3},{3,2},{4,5},{5,4},{6,7},{7,6},{8,9},{9,8},{10,11... | collective-permute-start | bytes 9437192 | tf_op jit(solution)/shard_map/ppermute | solution.py:44
  223.3 5.7 %collective-permute-start.25 = (bf16[8,768,256]{2,1,0:T(8,128)(2,1)S(1)}, bf16[8,768,256]{2,1,0:T(8,128)(2,1)S(1)}, u32[]{:S(2)}, u32[]{:S(2)}) collective-permute-start(bf16[8,768,256]{2,1,0:T(8,128)(2,1)S(1)} %shard_map.231), channel_id=1, source_target_pairs={{0,1},{1,0},{2,3},{3,2},{4,5},{5,4},{6,7},{7,6},{8,9},{9,8},{10,11... | collective-permute-start | bytes 9437192 | tf_op jit(solution)/shard_map/ppermute | solution.py:44
  308.1 4.5 %collective-permute-start.26 = (bf16[8,256,256]{2,1,0:T(8,128)(2,1)S(1)}, bf16[8,256,256]{2,1,0:T(8,128)(2,1)S(1)}, u32[]{:S(2)}, u32[]{:S(2)}) collective-permute-start(bf16[8,256,256]{2,1,0:T(8,128)(2,1)S(1)} %all_to_all.45.own_ref), channel_id=1, source_target_pairs={{0,1},{1,0},{2,3},{3,2},{4,5},{5,4},{6,7},{7,6},{8,9},{9,8},{10,11... | collective-permute-start | bytes 3145736 | tf_op jit(solution)/shard_map/ppermute | solution.py:44
  (30 other events, 257.3 us)
